TPU v7x, 512 devices: a whole 4x8x8 slice. The times are simulated.
512 devices in a mesh: row: 16 (over y, core), col: 32 (over x, z).
Axes of the slice: x: 4, y: 8, z: 8, core: 2. Of those that a mesh axis runs over, the one named last changes fastest.
Arguments:
- matrix: bfloat16 [8192, 131072], P('row', 'col'), may hold values from -6 to 6
- sketch: bfloat16 [131072, 128], P('col'), may hold values from -0.015625 to 0.015625
Outputs:
- basis: bfloat16 [8192, 128], P('row')
- projected: bfloat16 [128, 131072], P(None, 'col')
All inputs are finite; a program needn't handle non-finite values.
Results may differ from a plain program's by a relative error of at most 0.0048.
Values may be sent and summed in bfloat16 or wider, within the bound.
No kernel may reach another device: no remote copies, remote signals or barrier semaphores. Data moves between devices by JAX's collectives and lax.ppermute only.
A program may use at most 64 MiB of HBM per device.

v0:
```python
import jax
import jax.numpy as jnp
from jax import lax
from jax.sharding import PartitionSpec as P


def gram_of(rows):
    return jnp.dot(rows.T, rows, precision=lax.Precision.HIGHEST)


def solve_rows(lower, rows):
    solved = lax.linalg.triangular_solve(lower, rows, left_side=False, lower=True, transpose_a=True)
    return solved.astype(jnp.bfloat16)


def full_sketch(partial_value):
    return lax.psum(partial_value, "col")


def local(matrix, sketch):
    partial_value = jnp.dot(matrix, sketch, preferred_element_type=jnp.float32)
    sampled = full_sketch(partial_value)
    gram = lax.psum(gram_of(sampled), "row")
    lower = jnp.linalg.cholesky(gram)
    basis = solve_rows(lower, sampled)
    terms = jnp.dot(basis.T, matrix, preferred_element_type=jnp.float32)
    projected = lax.psum(terms, "row").astype(jnp.bfloat16)
    return (basis, projected)


def solution(mesh):
    return jax.shard_map(
        local,
        mesh=mesh,
        in_specs=(P("row", "col"), P("col", None)),
        out_specs=(P("row", None), P(None, "col")),
        check_vma=False,
    )
```

profile of v0, /device:TPU:1, one launch (start us, length us, event | category | flops | bytes accessed | tf_op | source)
XLA Modules:
  0.0 370.0 jit_solution(17476409709667343630)
XLA Ops:
  7.2 0.0 copy-start
  7.2 0.0 all-reduce.4.cloned.1.call-start
  7.2 1.2 copy-done
  8.4 4.1 %fusion.3 = f32[512,128]{1,0:T(8,128)} fusion(bf16[512,4096]{1,0:T(8,128)(2,1)} %param.2, bf16[4096,128]{1,0:T(8,128)(2,1)S(1)} %copy-done), kind=kOutput, calls=%fused_computation.10 | convolution fusion | flops 536870912 | bytes 5505024 | tf_op jit(solution)/shard_map/dot_general | solution.py:21
  12.5 0.0 all-reduce.4.cloned.1.call-update
  12.6 0.0 all-reduce.6.cloned.1.call-start
  12.6 156.6 %all-reduce.4.cloned.1.call-done = f32[512,128]{1,0:T(8,128)} async-done(((f32[512,128]{1,0:T(8,128)}), f32[512,128]{1,0:T(8,128)}) %all-reduce.4.cloned.1.call-update) | async-done | bytes 262160 | tf_op jit(solution)/shard_map/psum | solution.py:17
  169.2 2.2 fusion.4
  171.5 0.0 all-reduce.6.cloned.1.call-update
  171.5 106.5 %all-reduce.6.cloned.1.call-done = f32[128,128]{0,1:T(8,128)} async-done(((f32[128,128]{0,1:T(8,128)}), f32[128,128]{0,1:T(8,128)}) %all-reduce.6.cloned.1.call-update) | async-done | bytes 65552 | tf_op jit(solution)/shard_map/psum | solution.py:23
  278.0 0.9 copy.5
  279.0 0.9 fusion.2
  279.8 11.7 %cholesky.16 = f32[128,128]{1,0:T(8,128)S(1)} custom-call(f32[128,128]{1,0:T(8,128)S(1)} %fusion.2), custom_call_target="Cholesky" | custom-call | tf_op jit(solution)/shard_map/jit(cholesky)/cholesky | solution.py:24
  291.6 0.6 compare_reduce_fusion
  292.2 0.7 fusion
  292.9 9.8 %custom-call.6 = f32[1,128,128]{1,2,0:T(8,128)S(1)} custom-call(f32[1,128,128]{2,1,0:T(8,128)S(1)} %fusion), custom_call_target="InvertDiagBlocksLowerTriangular" | custom-call | tf_op jit(solution)/shard_map/triangular_solve | solution.py:12
  302.7 1.3 convolution_convert_fusion
  304.0 0.0 copy-start.1
  304.0 3.0 fusion.5
  307.0 56.1 %all-reduce.7 = bf16[128,4096]{1,0:T(8,128)(2,1)} all-reduce(f32[128,4096]{1,0:T(8,128)S(1)} %fusion.5), channel_id=1, replica_groups=mesh['row'=16,'col'=32] {'row'}, use_global_device_ids=true, to_apply=%region_4.5 | all-reduce | flops 524288 | bytes 3145728 | tf_op jit(solution)/shard_map/psum | solution.py:27
  363.1 0.0 copy-done.1
  (1 shorter events, 0.0 us)
Async XLA Ops:
  7.2 1.2 copy-start
  7.2 162.1 %all-reduce.4.cloned.1.call-start = ((), (), s32[]{:S(2)}) async-start(), calls=%async_computation | async-start | bytes 524288 | tf_op jit(solution)/shard_map/psum | solution.py:17
  12.6 265.5 %all-reduce.6.cloned.1.call-start = ((), (), s32[]{:S(2)}) async-start(), calls=%async_computation.1 | async-start | bytes 131072 | tf_op jit(solution)/shard_map/psum | solution.py:23
  304.0 59.1 %copy-start.1 = (bf16[512,128]{1,0:T(8,128)(2,1)}, bf16[512,128]{1,0:T(8,128)(2,1)S(1)}, u32[]{:S(2)}) copy-start(bf16[512,128]{1,0:T(8,128)(2,1)S(1)} %convolution_convert_fusion) | copy-start | bytes 393220
Sparse Core Ops, SparseCore 0:
  12.7 156.5 all-reduce.3
  172.1 105.8 all-reduce.5
where the time goes:
time: 372 us; the launch traced here: 370 us
  waiting for transfers between devices  263 us (71%)
  blocking collectives  56.1 us (15%)
  other arithmetic  23.7 us (6%)
  between operations  14.1 us (4%)
  matrix products  10.7 us (3%)
    psum x1, waiting for transfers between devices, full_sketch(): return lax.psum(partial_value, 'col')  157 us
    psum x1, waiting for transfers between devices, local(): gram = lax.psum(gram_of(sampled), 'row')  107 us
    psum x1, blocking collectives, local(): projected = lax.psum(terms, 'row').astype(jnp.bfloat16)  56.1 us
    another operation x3, other arithmetic, local(): lower = jnp.linalg.cholesky(gram)  12.4 us
    another operation x2, other arithmetic, solve_rows(): lax.linalg.triangular_solve(lower, rows, left_side=False, lower=True, tra...  10.5 us
  transfers between devices with their start and end apart: 2, of which 2 were waited for; matrix products, arithmetic and copies ran while one was open for 0% of the time, Pallas kernels for 0%

commit v1 on v0

v1 whole, which is shorter than its diff:
```python
import jax
import jax.numpy as jnp
from jax import lax
from jax.experimental import pallas as pl
from jax.experimental.pallas import tpu as pltpu
from jax.sharding import PartitionSpec as P

K = 128
T = 8
NP = K // T
NX, NY, NZ = 4, 8, 8
NROW, NCOL = 16, 32
F32 = jnp.float32
BF16 = jnp.bfloat16
HIGH = lax.Precision.HIGHEST


def sub_row(x, i):
    return jnp.broadcast_to(x[i : i + 1, :], (T, K))


def lane_col(x, i):
    return jnp.broadcast_to(x[:, i : i + 1], (T, K))


def chol_inv_kernel(g_ref, o_ref):
    sub = lax.broadcasted_iota(jnp.int32, (T, K), 0)
    lane = lax.broadcasted_iota(jnp.int32, (T, K), 1)
    a = [g_ref[p * T : (p + 1) * T, :] for p in range(NP)]
    for k in range(NP):
        lo = k * T
        inside = (lane >= lo) & (lane < lo + T)
        c = [lane_col(a[k], lo + j) for j in range(T)]
        x = jnp.where(inside, jnp.where(lane - lo == sub, 1.0, 0.0), a[k])
        u = x
        dvec = c[0]
        for j in range(T):
            at = sub == j
            d = sub_row(c[j], j)
            r = 1.0 / d
            u = jnp.where(at, x, u)
            dvec = jnp.where(at, d, dvec)
            xj = sub_row(x, j)
            cj = c[j]
            x = jnp.where(at, xj * r, x - (cj * xj) * r)
            for l in range(j + 1, T):
                cl = sub_row(c[l], j)
                c[l] = jnp.where(at, cl * r, c[l] - (cj * cl) * r)
        rows = [sub_row(x, j) for j in range(T)]
        for p in range(k + 1, NP):
            terms = [lane_col(a[p], lo + j) * rows[j] for j in range(T)]
            while len(terms) > 1:
                terms = [terms[i] + terms[i + 1] for i in range(0, len(terms), 2)]
            a[p] = jnp.where(inside, 0.0, a[p]) - terms[0]
        o_ref[lo : lo + T, :] = jnp.where(lane <= lo + sub, u * lax.rsqrt(dvec), 0.0)


def chol_inv(gram):
    return pl.pallas_call(
        chol_inv_kernel,
        out_shape=jax.ShapeDtypeStruct((K, K), F32),
        name="chol_inv",
    )(gram)


def w_kernel(core_ref, s_ref, m_ref, own_ref, other_ref):
    turned = s_ref[...].T
    high = turned.astype(BF16)
    low = (turned - high.astype(F32)).astype(BF16)
    hl = jnp.concatenate([high, low], axis=0)
    width = own_ref.shape[2]
    core = core_ref[0]
    for half, out_ref in ((1 - core, other_ref), (core, own_ref)):
        for y in range(NY):
            at = pl.multiple_of((half * NY + y) * width, width)
            w = jnp.dot(hl, m_ref[:, pl.ds(at, width)], preferred_element_type=F32)
            out_ref[y] = w[:K] + w[K:]


def sketch_rows(sampled, matrix, core):
    width = matrix.shape[1] // NROW
    vmem = pl.BlockSpec(memory_space=pltpu.VMEM)
    return pl.pallas_call(
        w_kernel,
        in_specs=[pl.BlockSpec(memory_space=pltpu.SMEM), vmem, vmem],
        out_specs=[vmem, vmem],
        out_shape=[jax.ShapeDtypeStruct((NY, K, width), F32)] * 2,
        cost_estimate=pl.CostEstimate(
            flops=4 * K * matrix.size, bytes_accessed=9 << 20, transcendentals=0
        ),
        compiler_params=pltpu.CompilerParams(vmem_limit_bytes=40 << 20),
        name="sketch_rows",
    )(core.astype(jnp.int32).reshape(1), sampled, matrix)


def finish_kernel(inv_ref, parts_ref, out_ref):
    total = parts_ref[0]
    for k in range(1, NY):
        total = total + parts_ref[k]
    piece = jnp.dot(inv_ref[...], total, precision=HIGH, preferred_element_type=F32).astype(BF16)
    for k in range(NY):
        out_ref[k] = piece


def finish(inverse, parts):
    return pl.pallas_call(
        finish_kernel,
        out_shape=jax.ShapeDtypeStruct(parts.shape, BF16),
        name="finish",
    )(inverse, parts)


def place_kernel(core_ref, own_ref, other_ref, out_ref):
    width = own_ref.shape[2]
    core = core_ref[0]
    for half, ref in ((core, own_ref), (1 - core, other_ref)):
        for y in range(NY):
            at = pl.multiple_of((half * NY + y) * width, width)
            out_ref[:, pl.ds(at, width)] = ref[y]


def place(own, other, core):
    vmem = pl.BlockSpec(memory_space=pltpu.VMEM)
    return pl.pallas_call(
        place_kernel,
        in_specs=[pl.BlockSpec(memory_space=pltpu.SMEM), vmem, vmem],
        out_specs=vmem,
        out_shape=jax.ShapeDtypeStruct((K, NROW * own.shape[2]), BF16),
        name="place",
    )(core.astype(jnp.int32).reshape(1), own, other)


SWAP = [(i, i ^ 1) for i in range(NROW)]
Y_GROUPS = [[2 * k + core for k in range(NY)] for core in range(2)]
Z_GROUPS = [[x * NZ + k for k in range(NZ)] for x in range(NX)]


def spread(block, n):
    return jnp.broadcast_to(block[None], (n, *block.shape))


def local(matrix, sketch):
    core = lax.axis_index("row") % 2
    z = lax.axis_index("col") % NZ
    rows = matrix.shape[0]

    partial_value = jnp.dot(matrix, sketch, preferred_element_type=F32)
    parts = lax.all_to_all(partial_value.reshape(NCOL, rows // NCOL, K), "col", 0, 0)
    share = jnp.sum(parts, axis=0)
    sampled = lax.all_to_all(spread(share, NCOL), "col", 0, 0).reshape(rows, K)

    gram = jnp.dot(sampled.T, sampled, precision=HIGH)
    strip = lax.dynamic_slice_in_dim(gram, z * (K // NZ), K // NZ, 0)
    strip = jnp.sum(lax.all_to_all(spread(strip, NROW), "row", 0, 0), axis=0)
    gram = lax.all_to_all(spread(strip, NZ), "col", 0, 0, axis_index_groups=Z_GROUPS)
    inverse = chol_inv(gram.reshape(K, K))

    own, other = sketch_rows(sampled, matrix, core)
    mine = own + lax.ppermute(other, "row", SWAP)
    parts = lax.all_to_all(mine, "row", 0, 0, axis_index_groups=Y_GROUPS)

    pieces = lax.all_to_all(finish(inverse, parts), "row", 0, 0, axis_index_groups=Y_GROUPS)
    basis = lax.dot_general(sampled, inverse, (((1,), (1,)), ((), ())), precision=HIGH).astype(BF16)
    return basis, place(pieces, lax.ppermute(pieces, "row", SWAP), core)


def solution(mesh):
    return jax.shard_map(
        local,
        mesh=mesh,
        in_specs=(P("row", "col"), P("col", None)),
        out_specs=(P("row", None), P(None, "col")),
        check_vma=False,
    )
```

time: 372 us -> 148 us (0.40)
  waiting for transfers between devices: 263 us -> 38.3 us
  other arithmetic: 23.7 us -> 2.39 us
  starting transfers between devices: 0.08 us -> 21.3 us
  between operations: 14.1 us -> 0.78 us
  Pallas kernels: 0 us -> 11.7 us
  matrix products: 10.7 us -> 5.9 us
  local copies, waits for them, and re-layouts: 2.11 us -> 6.54 us
  blocking collectives: 56.1 us -> 60.5 us
    psum x2 -> x0, waiting for transfers between devices: 263 us -> none  [the longest x1 157 us: full_sketch(): return lax.psum(partial_value, 'col')]
    all_to_all x0 -> x3, blocking collectives: none -> 60.5 us  [the longest x1 23.2 us: local(): lax.all_to_all(partial_value.reshape(NCOL, rows // NCOL, K), 'col', 0, 0)]
    psum x1 -> x0, blocking collectives: 56.1 us -> none  [local(): projected = lax.psum(terms, 'row').astype(jnp.bfloat16)]
    all_to_all x0 -> x3, waiting for transfers between devices: none -> 38.3 us  [the longest x1 23.3 us: local(): parts = lax.all_to_all(mine, 'row', 0, 0, axis_index_groups=Y_GROUPS)]
    another operation x5 -> x0, other arithmetic: 22.9 us -> none  [the longest x3 12.4 us: local(): lower = jnp.linalg.cholesky(gram)]
    all_to_all x0 -> x3, starting transfers between devices: none -> 13.2 us  [the longest x1 6.29 us: local(): sampled = lax.all_to_all(spread(share, NCOL), 'col', 0, 0).reshape(rows, K)]
    pallas_call x0 -> x4, Pallas kernels: none -> 11.7 us  [the longest x1 5.81 us: chol_inv(): pl.pallas_call(chol_inv_kernel, out_shape=jax.ShapeDtypeStruct((K, K), F3...]
    ppermute x0 -> x2, starting transfers between devices: none -> 8.13 us  [the longest x1 5.51 us: local(): mine = own + lax.ppermute(other, 'row', SWAP)]
  transfers between devices with their start and end apart: 2 -> 5, of which waited for: 2 -> 3; matrix products, arithmetic and copies ran while one was open for 0% -> 4% of each run, Pallas kernels for 0% -> 4%
where the time goes in v1:
time: 148 us
  blocking collectives  60.5 us (41%)
  waiting for transfers between devices  38.3 us (26%)
  starting transfers between devices  21.3 us (14%)
  Pallas kernels  11.7 us (8%)
  local copies, waits for them, and re-layouts  6.54 us (4%)
  matrix products  5.9 us (4%)
  other arithmetic  2.39 us (2%)
    all_to_all x1, waiting for transfers between devices, local(): parts = lax.all_to_all(mine, 'row', 0, 0, axis_index_groups=Y_GROUPS)  23.3 us
    all_to_all x1, blocking collectives, local(): lax.all_to_all(partial_value.reshape(NCOL, rows // NCOL, K), 'col', 0, 0)  23.2 us
    all_to_all x1, blocking collectives, local(): lax.all_to_all(finish(inverse, parts), 'row', 0, 0, axis_index_groups=Y_G...  21.1 us
    all_to_all x1, blocking collectives, local(): strip = jnp.sum(lax.all_to_all(spread(strip, NROW), 'row', 0, 0), axis=0)  16.2 us
    all_to_all x1, waiting for transfers between devices, local(): sampled = lax.all_to_all(spread(share, NCOL), 'col', 0, 0).reshape(rows, K)  9.65 us
    all_to_all x1, starting transfers between devices, local(): sampled = lax.all_to_all(spread(share, NCOL), 'col', 0, 0).reshape(rows, K)  6.29 us
    pallas_call x1, Pallas kernels, chol_inv(): pl.pallas_call(chol_inv_kernel, out_shape=jax.ShapeDtypeStruct((K, K), F3...  5.81 us
    ppermute x1, starting transfers between devices, local(): mine = own + lax.ppermute(other, 'row', SWAP)  5.51 us
  transfers between devices with their start and end apart: 5, of which 3 were waited for; matrix products, arithmetic and copies ran while one was open for 4% of the time, Pallas kernels for 4%

profile of v1, /device:TPU:1, one launch (start us, length us, event | category | flops | bytes accessed | tf_op | source)
XLA Modules:
  0.0 147.5 jit_solution(7644966537515032356)
XLA Ops:
  0.6 0.0 copy-start
  0.6 1.2 copy-done
  1.9 3.4 %fusion = f32[512,128]{1,0:T(8,128)S(1)} fusion(bf16[512,4096]{1,0:T(8,128)(2,1)} %m_ref.1, bf16[4096,128]{1,0:T(8,128)(2,1)S(1)} %copy-done), kind=kOutput, calls=%fused_computation.3 | convolution fusion | flops 536870912 | bytes 5505024 | tf_op jit(solution)/shard_map/dot_general | solution.py:147
  5.3 23.2 %all_to_all.30 = f32[32,16,128]{2,1,0:T(8,128)S(1)} all-to-all(f32[32,16,128]{2,1,0:T(8,128)S(1)} %bitcast.14), channel_id=1, replica_groups=mesh['row'=16,'col'=32] {'col'}, dimensions={0} | all-to-all | bytes 524288 | tf_op jit(solution)/shard_map/all_to_all | solution.py:148
  28.5 0.7 broadcast_in_dim.6
  29.3 6.3 %all-to-all-start.1 = ((f32[32,16,128]{2,1,0:T(8,128)}), f32[32,16,128]{2,1,0:T(8,128)S(1)}, u32[]{:S(2)}, u32[]{:S(2)}) async-start(f32[32,16,128]{2,1,0:T(8,128)} %broadcast_in_dim.6), calls=%async_computation.1 | async-start | bytes 524288 | tf_op jit(solution)/shard_map/all_to_all | solution.py:150
  35.6 9.6 %all-to-all-done.1 = f32[32,16,128]{2,1,0:T(8,128)S(1)} async-done(((f32[32,16,128]{2,1,0:T(8,128)}), f32[32,16,128]{2,1,0:T(8,128)S(1)}, u32[]{:S(2)}, u32[]{:S(2)}) %all-to-all-start.1) | async-done | bytes 262176 | tf_op jit(solution)/shard_map/all_to_all | solution.py:150
  45.2 0.0 copy-start.1
  45.2 2.2 %copy-done.1 = bf16[512,4096]{1,0:T(8,128)(2,1)S(1)} copy-done((bf16[512,4096]{1,0:T(8,128)(2,1)S(1)}, bf16[512,4096]{1,0:T(8,128)(2,1)}, u32[]{:S(2)}) %copy-start.1) | copy-done | bytes 4194328
  47.4 1.3 sketch_rows.1
  48.7 5.5 %collective-permute-start = (f32[8,128,256]{2,1,0:T(8,128)S(1)}, f32[8,128,256]{2,1,0:T(8,128)}, u32[]{:S(2)}, u32[]{:S(2)}) collective-permute-start(f32[8,128,256]{2,1,0:T(8,128)S(1)} %get-tuple-element.5), channel_id=1, source_target_pairs={{0,32},{32,0},{64,96},{96,64},{128,160},{160,128},{192,224},{224,1... | collective-permute-start | bytes 3145736 | tf_op jit(solution)/shard_map/ppermute | solution.py:159
  54.2 0.6 convolution_bitcast_fusion
  54.9 16.2 %all_to_all.31 = f32[16,16,128]{2,1,0:T(8,128)S(1)} all-to-all(f32[16,16,128]{2,1,0:T(8,128)S(1)} %broadcast_in_dim.7), channel_id=1, replica_groups=mesh['row'=16,'col'=32] {'row'}, dimensions={0} | all-to-all | bytes 262144 | tf_op jit(solution)/shard_map/all_to_all | solution.py:154
  71.1 0.6 broadcast_in_dim.8
  71.7 3.4 %all-to-all-start.3 = ((f32[8,16,128]{2,1,0:T(8,128)}), f32[8,16,128]{2,1,0:T(8,128)S(1)}, u32[]{:S(2)}, u32[]{:S(2)}) async-start(f32[8,16,128]{2,1,0:T(8,128)} %broadcast_in_dim.8), calls=%async_computation.3 | async-start | bytes 131072 | tf_op jit(solution)/shard_map/all_to_all | solution.py:155
  75.1 0.0 collective-permute-done
  75.1 2.3 %add.16 = f32[8,128,256]{2,1,0:T(8,128)} add(f32[8,128,256]{2,1,0:T(8,128)S(1)} %get-tuple-element.4, f32[8,128,256]{2,1,0:T(8,128)} %collective-permute-done) | non-fusion elementwise | flops 262144 | bytes 3145728 | tf_op jit(solution)/shard_map/add | solution.py:159
  77.4 5.4 %all-to-all-done.3 = f32[8,16,128]{2,1,0:T(8,128)S(1)} async-done(((f32[8,16,128]{2,1,0:T(8,128)}), f32[8,16,128]{2,1,0:T(8,128)S(1)}, u32[]{:S(2)}, u32[]{:S(2)}) %all-to-all-start.3) | async-done | bytes 65568 | tf_op jit(solution)/shard_map/all_to_all | solution.py:155
  82.8 0.0 copy-start.5
  82.8 3.6 %all-to-all-start.4 = ((f32[8,128,256]{2,1,0:T(8,128)}), f32[8,128,256]{2,1,0:T(8,128)S(1)}, u32[]{:S(2)}, u32[]{:S(2)}) async-start(f32[8,128,256]{2,1,0:T(8,128)} %add.16), calls=%async_computation.4 | async-start | bytes 2097152 | tf_op jit(solution)/shard_map/all_to_all | solution.py:160
  86.3 0.0 copy-done.5
  86.4 5.8 %chol_inv.1.inv_ref = f32[128,128]{1,0:T(8,128)} custom-call(f32[128,128]{1,0:T(8,128)} %bitcast.15), custom_call_target="tpu_custom_call" | custom-call | tf_op jit(solution)/shard_map/chol_inv/pallas_call | solution.py:59
  92.2 23.3 %all-to-all-done.4.parts_ref = f32[8,128,256]{2,1,0:T(8,128)S(1)} async-done(((f32[8,128,256]{2,1,0:T(8,128)}), f32[8,128,256]{2,1,0:T(8,128)S(1)}, u32[]{:S(2)}, u32[]{:S(2)}) %all-to-all-start.4) | async-done | bytes 1048608 | tf_op jit(solution)/shard_map/all_to_all | solution.py:160
  115.5 0.0 copy-start.2
  115.5 1.0 copy-done.2
  116.5 2.4 %finish.1 = bf16[8,128,256]{2,1,0:T(8,128)(2,1)} custom-call(f32[128,128]{1,0:T(8,128)} %chol_inv.1.inv_ref, f32[8,128,256]{2,1,0:T(8,128)} %copy-done.2), custom_call_target="tpu_custom_call" | custom-call | tf_op jit(solution)/shard_map/finish/pallas_call | solution.py:106
  118.8 21.1 %all_to_all.32.own_ref = bf16[8,128,256]{2,1,0:T(8,128)(2,1)S(1)} all-to-all(bf16[8,128,256]{2,1,0:T(8,128)(2,1)} %finish.1), channel_id=1, replica_groups={{0,64,128,192,256,320,384,448},{32,96,160,224,288,352,416,480},{1,65,12..., dimensions={0} | all-to-all | bytes 1048576 | tf_op jit(solution)/shard_map/all_to_all | solution.py:162
  139.9 0.0 copy-start.3
  139.9 2.6 %collective-permute-start.1 = (bf16[8,128,256]{2,1,0:T(8,128)(2,1)S(1)}, bf16[8,128,256]{2,1,0:T(8,128)(2,1)S(1)}, u32[]{:S(2)}, u32[]{:S(2)}) collective-permute-start(bf16[8,128,256]{2,1,0:T(8,128)(2,1)S(1)} %all_to_all.32.own_ref), channel_id=1, source_target_pairs={{0,32},{32,0},{64,96},{96,64},{128,160},{160,128},{192,224},{224,1... | collective-permute-start | bytes 1572872 | tf_op jit(solution)/shard_map/ppermute | solution.py:164
  142.6 1.9 %convolution_convert_fusion = bf16[512,128]{1,0:T(8,128)(2,1)} fusion(f32[512,128]{1,0:T(8,128)S(1)} %bitcast.13, f32[128,128]{1,0:T(8,128)} %chol_inv.1.inv_ref), kind=kOutput, calls=%fused_computation | convolution fusion | flops 100728832 | bytes 458752 | tf_op jit(solution)/shard_map/dot_general | solution.py:163
  144.5 0.0 collective-permute-done.1.other_ref
  144.5 0.0 copy-done.3
  144.5 0.0 copy-start.4
  144.5 0.8 copy-done.4
  145.2 2.3 %place.1 = bf16[128,4096]{1,0:T(8,128)(2,1)} custom-call(s32[1]{0:T(128)} %bitcast.4.core_ref, bf16[8,128,256]{2,1,0:T(8,128)(2,1)} %copy-done.3, bf16[8,128,256]{2,1,0:T(8,128)(2,1)} %copy-done.4), custom_call_target="tpu_custom_call" | custom-call | tf_op jit(solution)/shard_map/place/pallas_call | solution.py:124
  (4 shorter events, 0.1 us)
Async XLA Ops:
  0.6 1.2 copy-start
  29.3 16.0 %all-to-all-start.1 = ((f32[32,16,128]{2,1,0:T(8,128)}), f32[32,16,128]{2,1,0:T(8,128)S(1)}, u32[]{:S(2)}, u32[]{:S(2)}) async-start(f32[32,16,128]{2,1,0:T(8,128)} %broadcast_in_dim.6), calls=%async_computation.1 | async-start | bytes 524288 | tf_op jit(solution)/shard_map/all_to_all | solution.py:150
  45.2 2.2 %copy-start.1 = (bf16[512,4096]{1,0:T(8,128)(2,1)S(1)}, bf16[512,4096]{1,0:T(8,128)(2,1)}, u32[]{:S(2)}) copy-start(bf16[512,4096]{1,0:T(8,128)(2,1)} %m_ref.1) | copy-start | bytes 12582916
  48.7 26.4 %collective-permute-start = (f32[8,128,256]{2,1,0:T(8,128)S(1)}, f32[8,128,256]{2,1,0:T(8,128)}, u32[]{:S(2)}, u32[]{:S(2)}) collective-permute-start(f32[8,128,256]{2,1,0:T(8,128)S(1)} %get-tuple-element.5), channel_id=1, source_target_pairs={{0,32},{32,0},{64,96},{96,64},{128,160},{160,128},{192,224},{224,1... | collective-permute-start | bytes 3145736 | tf_op jit(solution)/shard_map/ppermute | solution.py:159
  71.7 11.1 %all-to-all-start.3 = ((f32[8,16,128]{2,1,0:T(8,128)}), f32[8,16,128]{2,1,0:T(8,128)S(1)}, u32[]{:S(2)}, u32[]{:S(2)}) async-start(f32[8,16,128]{2,1,0:T(8,128)} %broadcast_in_dim.8), calls=%async_computation.3 | async-start | bytes 131072 | tf_op jit(solution)/shard_map/all_to_all | solution.py:155
  82.8 3.6 %copy-start.5 = (f32[8,16,128]{2,1,0:T(8,128)}, f32[8,16,128]{2,1,0:T(8,128)S(1)}, u32[]{:S(2)}) copy-start(f32[8,16,128]{2,1,0:T(8,128)S(1)} %all-to-all-done.3) | copy-start | bytes 196612
  82.8 32.7 %all-to-all-start.4 = ((f32[8,128,256]{2,1,0:T(8,128)}), f32[8,128,256]{2,1,0:T(8,128)S(1)}, u32[]{:S(2)}, u32[]{:S(2)}) async-start(f32[8,128,256]{2,1,0:T(8,128)} %add.16), calls=%async_computation.4 | async-start | bytes 2097152 | tf_op jit(solution)/shard_map/all_to_all | solution.py:160
  115.5 1.0 copy-start.2
  139.9 4.5 %copy-start.3 = (bf16[8,128,256]{2,1,0:T(8,128)(2,1)}, bf16[8,128,256]{2,1,0:T(8,128)(2,1)S(1)}, u32[]{:S(2)}) copy-start(bf16[8,128,256]{2,1,0:T(8,128)(2,1)S(1)} %all_to_all.32.own_ref) | copy-start | bytes 1572868
  139.9 4.5 %collective-permute-start.1 = (bf16[8,128,256]{2,1,0:T(8,128)(2,1)S(1)}, bf16[8,128,256]{2,1,0:T(8,128)(2,1)S(1)}, u32[]{:S(2)}, u32[]{:S(2)}) collective-permute-start(bf16[8,128,256]{2,1,0:T(8,128)(2,1)S(1)} %all_to_all.32.own_ref), channel_id=1, source_target_pairs={{0,32},{32,0},{64,96},{96,64},{128,160},{160,128},{192,224},{224,1... | collective-permute-start | bytes 1572872 | tf_op jit(solution)/shard_map/ppermute | solution.py:164
  144.5 0.8 copy-start.4

commit v2 on v1

v2 whole, which is shorter than its diff:
```python
import jax
import jax.numpy as jnp
from jax import lax
from jax.experimental import pallas as pl
from jax.experimental.pallas import tpu as pltpu
from jax.sharding import PartitionSpec as P

K = 128
T = 8
NP = K // T
NX, NY, NZ = 4, 8, 8
NROW, NCOL = 16, 32
F32 = jnp.float32
BF16 = jnp.bfloat16
HIGH = lax.Precision.HIGHEST


def room(mib):
    return pltpu.CompilerParams(vmem_limit_bytes=mib << 20)


def sub_row(x, i):
    return jnp.broadcast_to(x[i : i + 1, :], (T, K))


def lane_col(x, i):
    return jnp.broadcast_to(x[:, i : i + 1], (T, K))


def chol_inv_kernel(g_ref, o_ref):
    sub = lax.broadcasted_iota(jnp.int32, (T, K), 0)
    lane = lax.broadcasted_iota(jnp.int32, (T, K), 1)
    a = [g_ref[p * T : (p + 1) * T, :] for p in range(NP)]
    for k in range(NP):
        lo = k * T
        inside = (lane >= lo) & (lane < lo + T)
        c = [lane_col(a[k], lo + j) for j in range(T)]
        x = jnp.where(inside, jnp.where(lane - lo == sub, 1.0, 0.0), a[k])
        u = x
        dvec = c[0]
        for j in range(T):
            at = sub == j
            d = sub_row(c[j], j)
            r = 1.0 / d
            u = jnp.where(at, x, u)
            dvec = jnp.where(at, d, dvec)
            xj = sub_row(x, j)
            cj = c[j]
            x = jnp.where(at, xj * r, x - (cj * xj) * r)
            for l in range(j + 1, T):
                cl = sub_row(c[l], j)
                c[l] = jnp.where(at, cl * r, c[l] - (cj * cl) * r)
        rows = [sub_row(x, j) for j in range(T)]
        for p in range(k + 1, NP):
            terms = [lane_col(a[p], lo + j) * rows[j] for j in range(T)]
            while len(terms) > 1:
                terms = [terms[i] + terms[i + 1] for i in range(0, len(terms), 2)]
            a[p] = jnp.where(inside, 0.0, a[p]) - terms[0]
        o_ref[lo : lo + T, :] = jnp.where(lane <= lo + sub, u * lax.rsqrt(dvec), 0.0)


def chol_inv(gram):
    return pl.pallas_call(
        chol_inv_kernel,
        out_shape=jax.ShapeDtypeStruct((K, K), F32),
        compiler_params=room(4),
        name="chol_inv",
    )(gram)


HBM = pl.BlockSpec(memory_space=pltpu.HBM)
VMEM = pl.BlockSpec(memory_space=pltpu.VMEM)
SMEM = pl.BlockSpec(memory_space=pltpu.SMEM)


def scalar(value):
    return value.astype(jnp.int32).reshape(1)


def sketch_kernel(core_ref, m_ref, o_ref, p_ref, send_ref, sem):
    half = send_ref.shape[1]
    at = pl.multiple_of((1 - core_ref[0]) * half, half)
    copy = pltpu.make_async_copy(m_ref.at[:, pl.ds(at, half)], send_ref, sem)
    copy.start()
    p_ref[...] = jnp.dot(m_ref[...], o_ref[...], preferred_element_type=F32)
    copy.wait()


def sketch(matrix, omega, core):
    rows, cols = matrix.shape
    return pl.pallas_call(
        sketch_kernel,
        in_specs=[SMEM, VMEM, VMEM],
        out_specs=[VMEM, VMEM],
        out_shape=[
            jax.ShapeDtypeStruct((rows, K), F32),
            jax.ShapeDtypeStruct((rows, cols // 2), BF16),
        ],
        scratch_shapes=[pltpu.SemaphoreType.DMA],
        compiler_params=room(16),
        name="sketch",
    )(scalar(core), matrix, omega)


def share_kernel(parts_ref, out_ref):
    terms = [parts_ref[k] for k in range(parts_ref.shape[0])]
    while len(terms) > 1:
        terms = [terms[i] + terms[i + 1] for i in range(0, len(terms), 2)]
    for k in range(out_ref.shape[0]):
        out_ref[k] = terms[0]


def share(parts, copies):
    return pl.pallas_call(
        share_kernel,
        in_specs=[VMEM],
        out_specs=VMEM,
        out_shape=jax.ShapeDtypeStruct((copies, *parts.shape[1:]), F32),
        compiler_params=room(4),
        name="share",
    )(parts)


def w_kernel(core_ref, s_ref, m_ref, his_ref, gram_ref, w_ref):
    rows, half = his_ref.shape
    width = w_ref.shape[2]
    both = s_ref[...]
    gram_ref[...] = lax.dot_general(
        both, both, (((0,), (0,)), ((), ())), precision=HIGH, preferred_element_type=F32
    )
    core = core_ref[0]
    terms = []
    for who in (core, 1 - core):
        turned = s_ref[pl.ds(pl.multiple_of(who * rows, rows), rows), :].T
        high = turned.astype(BF16)
        low = (turned - high.astype(F32)).astype(BF16)
        terms.append(jnp.concatenate([high, low], axis=0))
    for y in range(NY):
        at = pl.multiple_of(core * half + y * width, width)
        w = jnp.dot(terms[0], m_ref[:, pl.ds(at, width)], preferred_element_type=F32)
        cut = slice(y * width, (y + 1) * width)
        w = w + jnp.dot(terms[1], his_ref[:, cut], preferred_element_type=F32)
        w_ref[y] = w[:K] + w[K:]


def sketch_rows(both, matrix, his, core):
    width = his.shape[1] // NY
    return pl.pallas_call(
        w_kernel,
        in_specs=[SMEM, VMEM, VMEM, VMEM],
        out_specs=[VMEM, VMEM],
        out_shape=[
            jax.ShapeDtypeStruct((K, K), F32),
            jax.ShapeDtypeStruct((NY, K, width), F32),
        ],
        compiler_params=room(20),
        name="sketch_rows",
    )(scalar(core), both, matrix, his)


def finish_kernel(inv_ref, parts_ref, out_ref, held, sems):
    copies = [pltpu.make_async_copy(parts_ref.at[k], held.at[k], sems.at[k]) for k in range(NY)]
    for copy in copies:
        copy.start()
    copies[0].wait()
    total = held[0]
    for k in range(1, NY):
        copies[k].wait()
        total = total + held[k]
    piece = jnp.dot(inv_ref[...], total, precision=HIGH, preferred_element_type=F32).astype(BF16)
    for k in range(NY):
        out_ref[k] = piece


def finish(inverse, parts):
    return pl.pallas_call(
        finish_kernel,
        in_specs=[VMEM, pl.BlockSpec(memory_space=pl.ANY)],
        out_specs=VMEM,
        out_shape=jax.ShapeDtypeStruct(parts.shape, BF16),
        scratch_shapes=[pltpu.VMEM(parts.shape, F32), pltpu.SemaphoreType.DMA((NY,))],
        compiler_params=room(8),
        name="finish",
    )(inverse, parts)


def place_kernel(core_ref, own_ref, other_ref, out_ref, sems):
    width = own_ref.shape[2]
    core = core_ref[0]
    copies = []
    for i, (half, ref) in enumerate(((core, own_ref), (1 - core, other_ref))):
        for y in range(NY):
            at = pl.multiple_of((half * NY + y) * width, width)
            copies.append(
                pltpu.make_async_copy(ref.at[y], out_ref.at[:, pl.ds(at, width)], sems.at[i, y])
            )
    for copy in copies:
        copy.start()
    for copy in copies:
        copy.wait()


def place(own, other, core):
    anywhere = pl.BlockSpec(memory_space=pl.ANY)
    return pl.pallas_call(
        place_kernel,
        in_specs=[SMEM, anywhere, anywhere],
        out_specs=HBM,
        out_shape=jax.ShapeDtypeStruct((K, NROW * own.shape[2]), BF16),
        scratch_shapes=[pltpu.SemaphoreType.DMA((2, NY))],
        compiler_params=room(4),
        name="place",
    )(scalar(core), own, other)


SWAP = [(i, i ^ 1) for i in range(NROW)]
Y_GROUPS = [[2 * k + core for k in range(NY)] for core in range(2)]
CHIP_GROUPS = [
    [(2 * y + core) * NCOL + c for core in range(2) for c in range(NCOL)] for y in range(NY)
]


def local(matrix, omega):
    core = lax.axis_index("row") % 2
    rows = matrix.shape[0]

    partial_value, send = sketch(matrix, omega, core)
    parts = lax.all_to_all(partial_value.reshape(NCOL, rows // NCOL, K), "col", 0, 0)
    his = lax.ppermute(send, "row", SWAP)
    both = lax.all_to_all(
        share(parts, 2 * NCOL), ("row", "col"), 0, 0, axis_index_groups=CHIP_GROUPS
    ).reshape(2 * rows, K)

    gram, w = sketch_rows(both, matrix, his, core)
    parts = lax.all_to_all(w, "row", 0, 0, axis_index_groups=Y_GROUPS)
    for step in (1, 2, 4):
        gram = gram + lax.ppermute(gram, "row", [(i, i ^ (2 * step)) for i in range(NROW)])
    inverse = chol_inv(gram)

    pieces = lax.all_to_all(finish(inverse, parts), "row", 0, 0, axis_index_groups=Y_GROUPS)
    sampled = lax.dynamic_slice_in_dim(both, core * rows, rows, 0)
    basis = lax.dot_general(sampled, inverse, (((1,), (1,)), ((), ())), precision=HIGH).astype(BF16)
    return basis, place(pieces, lax.ppermute(pieces, "row", SWAP), core)


def solution(mesh):
    return jax.shard_map(
        local,
        mesh=mesh,
        in_specs=(P("row", "col"), P("col", None)),
        out_specs=(P("row", None), P(None, "col")),
        check_vma=False,
    )
```

time: 148 us -> 145 us (0.980)
  starting transfers between devices: 21.3 us -> 39.1 us
  waiting for transfers between devices: 38.3 us -> 23.7 us
  matrix products: 5.9 us -> 1.04 us
  blocking collectives: 60.5 us -> 64.8 us
  local copies, waits for them, and re-layouts: 6.54 us -> 3.41 us
  other arithmetic: 2.39 us -> 0.03 us
    all_to_all x3 -> x1, waiting for transfers between devices: 38.3 us -> 0.01 us  [local(): parts = lax.all_to_all(w, 'row', 0, 0, axis_index_groups=Y_GROUPS)]
    ppermute x1 -> x4, waiting for transfers between devices: 0.01 us -> 23.3 us  [the longest x3 23.3 us: local(): lax.ppermute(gram, 'row', [(i, i ^ 2 * step) for i in range(NROW)])]
    ppermute x1 -> x4, starting transfers between devices: 5.51 us -> 24.9 us  [the longest x3 16.1 us: local(): lax.ppermute(gram, 'row', [(i, i ^ 2 * step) for i in range(NROW)])]
    all_to_all x1, blocking collectives: 16.2 us -> 26.2 us  [local(): lax.all_to_all(share(parts, 2 * NCOL), ('row', 'col'), 0, 0, axis_index_g...]
    all_to_all x3 -> x1, starting transfers between devices: 13.2 us -> 6.82 us  [local(): parts = lax.all_to_all(w, 'row', 0, 0, axis_index_groups=Y_GROUPS)]
    all_to_all x1, blocking collectives: 23.2 us -> 17.6 us  [local(): lax.all_to_all(partial_value.reshape(NCOL, rows // NCOL, K), 'col', 0, 0)]
    ppermute x1, starting transfers between devices: 2.62 us -> 7.37 us  [local(): return (basis, place(pieces, lax.ppermute(pieces, 'row', SWAP), core))]
    dot_general x2 -> x0, matrix products: 4.02 us -> none  [the longest x1 3.43 us: local(): partial_value = jnp.dot(matrix, sketch, preferred_element_type=F32)]
  transfers between devices with their start and end apart: 5 -> 6, of which waited for: 3 -> 4; matrix products, arithmetic and copies ran while one was open for 4% -> 1% of each run, Pallas kernels for 4% -> 3%
where the time goes in v2:
time: 145 us
  blocking collectives  64.8 us (45%)
  starting transfers between devices  39.1 us (27%)
  waiting for transfers between devices  23.7 us (16%)
  Pallas kernels  11.7 us (8%)
  local copies, waits for them, and re-layouts  3.41 us (2%)
    all_to_all x1, blocking collectives, local(): lax.all_to_all(share(parts, 2 * NCOL), ('row', 'col'), 0, 0, axis_index_g...  26.2 us
    ppermute x3, waiting for transfers between devices, local(): lax.ppermute(gram, 'row', [(i, i ^ 2 * step) for i in range(NROW)])  23.3 us
    all_to_all x1, blocking collectives, local(): lax.all_to_all(finish(inverse, parts), 'row', 0, 0, axis_index_groups=Y_G...  20.9 us
    all_to_all x1, blocking collectives, local(): lax.all_to_all(partial_value.reshape(NCOL, rows // NCOL, K), 'col', 0, 0)  17.6 us
    ppermute x3, starting transfers between devices, local(): lax.ppermute(gram, 'row', [(i, i ^ 2 * step) for i in range(NROW)])  16.1 us
    ppermute x1, starting transfers between devices, local(): his = lax.ppermute(send, 'row', SWAP)  8.79 us
    ppermute x1, starting transfers between devices, local(): return (basis, place(pieces, lax.ppermute(pieces, 'row', SWAP), core))  7.37 us
    all_to_all x1, starting transfers between devices, local(): parts = lax.all_to_all(w, 'row', 0, 0, axis_index_groups=Y_GROUPS)  6.82 us
  transfers between devices with their start and end apart: 6, of which 4 were waited for; matrix products, arithmetic and copies ran while one was open for 1% of the time, Pallas kernels for 3%

profile of v2, /device:TPU:1, one launch (start us, length us, event | category | flops | bytes accessed | tf_op | source)
XLA Modules:
  0.0 144.5 jit_solution(14061609368257382864)
XLA Ops:
  0.6 0.0 copy-start
  0.7 2.2 %copy-done = bf16[512,4096]{1,0:T(8,128)(2,1)S(1)} copy-done((bf16[512,4096]{1,0:T(8,128)(2,1)S(1)}, bf16[512,4096]{1,0:T(8,128)(2,1)}, u32[]{:S(2)}) %copy-start) | copy-done | bytes 4194328
  2.8 0.0 copy-start.2
  2.8 1.2 copy-done.2
  4.1 0.0 copy-start.1
  4.1 1.8 %sketch.1 = (f32[512,128]{1,0:T(8,128)S(1)}, bf16[512,2048]{1,0:T(8,128)(2,1)S(1)}) custom-call(s32[1]{0:T(128)} %bitcast.core_ref, bf16[512,4096]{1,0:T(8,128)(2,1)S(1)} %copy-done, bf16[4096,128]{1,0:T(8,128)(2,1)S(1)} %copy-done.2), custom_call_target="tpu_custom_call" | custom-call | tf_op jit(solution)/shard_map/sketch/pallas_call | solution.py:91
  5.8 8.8 %collective-permute-start = (bf16[512,2048]{1,0:T(8,128)(2,1)S(1)}, bf16[512,2048]{1,0:T(8,128)(2,1)S(1)}, u32[]{:S(2)}, u32[]{:S(2)}) collective-permute-start(bf16[512,2048]{1,0:T(8,128)(2,1)S(1)} %get-tuple-element.7), channel_id=1, source_target_pairs={{0,32},{32,0},{64,96},{96,64},{128,160},{160,128},{192,224},{224,1... | collective-permute-start | bytes 6291464 | tf_op jit(solution)/shard_map/ppermute | solution.py:229
  14.6 17.6 %all_to_all.20.parts_ref = f32[32,16,128]{2,1,0:T(8,128)S(1)} all-to-all(f32[32,16,128]{2,1,0:T(8,128)S(1)} %bitcast.6), channel_id=1, replica_groups=mesh['row'=16,'col'=32] {'col'}, dimensions={0} | all-to-all | bytes 524288 | tf_op jit(solution)/shard_map/all_to_all | solution.py:228
  32.3 26.2 %all_to_all.21 = f32[64,16,128]{2,1,0:T(8,128)S(1)} all-to-all(f32[64,16,128]{2,1,0:T(8,128)S(1)} %share.1), channel_id=1, replica_groups={{0,1,2,3,4,5,6,7,8,9,10,11,12,13,14,15,16,17,18,19,20,21,22,23,24,25,26..., dimensions={0} | all-to-all | bytes 1048576 | tf_op jit(solution)/shard_map/all_to_all | solution.py:230
  58.5 0.0 collective-permute-done.his_ref
  58.5 0.0 copy-done.1
  58.5 2.7 %sketch_rows.1 = (f32[128,128]{1,0:T(8,128)S(1)}, f32[8,128,256]{2,1,0:T(8,128)}) custom-call(s32[1]{0:T(128)} %bitcast.core_ref, f32[1024,128]{1,0:T(8,128)S(1)} %bitcast.4, bf16[512,4096]{1,0:T(8,128)(2,1)S(1)} %copy-done.1, bf16[512,2048]{1,0:T(8,128)(2,1)S(1)} %collective-permute-done.his_ref), custom_call_target="tpu_custom_call" | custom-call | tf_op jit(solution)/shard_map/sketch_rows/pallas_call | solution.py:148
  61.2 6.8 %all-to-all-start.2 = ((f32[8,128,256]{2,1,0:T(8,128)}), f32[8,128,256]{2,1,0:T(8,128)S(1)}, u32[]{:S(2)}, u32[]{:S(2)}) async-start(f32[8,128,256]{2,1,0:T(8,128)} %get-tuple-element.9), calls=%async_computation.2 | async-start | bytes 2097152 | tf_op jit(solution)/shard_map/all_to_all | solution.py:235
  68.0 3.4 %collective-permute-start.1 = (f32[128,128]{1,0:T(8,128)S(1)}, f32[128,128]{1,0:T(8,128)S(1)}, u32[]{:S(2)}, u32[]{:S(2)}) collective-permute-start(f32[128,128]{1,0:T(8,128)S(1)} %get-tuple-element.8), channel_id=1, source_target_pairs={{0,64},{32,96},{64,0},{96,32},{128,192},{160,224},{192,128},{224,1... | collective-permute-start | bytes 196616 | tf_op jit(solution)/shard_map/ppermute | solution.py:237
  71.4 19.6 %collective-permute-done.1 = f32[128,128]{1,0:T(8,128)S(1)} collective-permute-done((f32[128,128]{1,0:T(8,128)S(1)}, f32[128,128]{1,0:T(8,128)S(1)}, u32[]{:S(2)}, u32[]{:S(2)}) %collective-permute-start.1) | collective-permute-done | bytes 65568 | tf_op jit(solution)/shard_map/ppermute | solution.py:237
  91.0 5.0 %collective-permute-start.2 = (f32[128,128]{1,0:T(8,128)S(1)}, f32[128,128]{1,0:T(8,128)S(1)}, u32[]{:S(2)}, u32[]{:S(2)}) collective-permute-start(f32[128,128]{1,0:T(8,128)S(1)} %add.18), channel_id=1, source_target_pairs={{0,128},{32,160},{64,192},{96,224},{128,0},{160,32},{192,64},{224,... | collective-permute-start | bytes 196616 | tf_op jit(solution)/shard_map/ppermute | solution.py:237
  96.0 2.0 %collective-permute-done.2 = f32[128,128]{1,0:T(8,128)S(1)} collective-permute-done((f32[128,128]{1,0:T(8,128)S(1)}, f32[128,128]{1,0:T(8,128)S(1)}, u32[]{:S(2)}, u32[]{:S(2)}) %collective-permute-start.2) | collective-permute-done | bytes 65568 | tf_op jit(solution)/shard_map/ppermute | solution.py:237
  98.0 7.8 %collective-permute-start.3 = (f32[128,128]{1,0:T(8,128)S(1)}, f32[128,128]{1,0:T(8,128)S(1)}, u32[]{:S(2)}, u32[]{:S(2)}) collective-permute-start(f32[128,128]{1,0:T(8,128)S(1)} %add.19), channel_id=1, source_target_pairs={{0,256},{32,288},{64,320},{96,352},{128,384},{160,416},{192,448},{... | collective-permute-start | bytes 196616 | tf_op jit(solution)/shard_map/ppermute | solution.py:237
  105.8 1.7 %collective-permute-done.3 = f32[128,128]{1,0:T(8,128)S(1)} collective-permute-done((f32[128,128]{1,0:T(8,128)S(1)}, f32[128,128]{1,0:T(8,128)S(1)}, u32[]{:S(2)}, u32[]{:S(2)}) %collective-permute-start.3) | collective-permute-done | bytes 65568 | tf_op jit(solution)/shard_map/ppermute | solution.py:237
  107.5 4.3 %chol_inv.1.inv_ref = f32[128,128]{1,0:T(8,128)S(1)} custom-call(f32[128,128]{1,0:T(8,128)S(1)} %add.20.g_ref), custom_call_target="tpu_custom_call" | custom-call | tf_op jit(solution)/shard_map/chol_inv/pallas_call | solution.py:63
  111.8 0.0 all-to-all-done.2.parts_ref
  111.9 1.7 %finish.1 = bf16[8,128,256]{2,1,0:T(8,128)(2,1)S(1)} custom-call(f32[128,128]{1,0:T(8,128)S(1)} %chol_inv.1.inv_ref, f32[8,128,256]{2,1,0:T(8,128)S(1)} %all-to-all-done.2.parts_ref), custom_call_target="tpu_custom_call" | custom-call | tf_op jit(solution)/shard_map/finish/pallas_call | solution.py:176
  113.6 20.9 %all_to_all.22.own_ref = bf16[8,128,256]{2,1,0:T(8,128)(2,1)S(1)} all-to-all(bf16[8,128,256]{2,1,0:T(8,128)(2,1)S(1)} %finish.1), channel_id=1, replica_groups={{0,64,128,192,256,320,384,448},{32,96,160,224,288,352,416,480},{1,65,12..., dimensions={0} | all-to-all | bytes 1048576 | tf_op jit(solution)/shard_map/all_to_all | solution.py:240
  134.5 7.4 %collective-permute-start.4 = (bf16[8,128,256]{2,1,0:T(8,128)(2,1)S(1)}, bf16[8,128,256]{2,1,0:T(8,128)(2,1)S(1)}, u32[]{:S(2)}, u32[]{:S(2)}) collective-permute-start(bf16[8,128,256]{2,1,0:T(8,128)(2,1)S(1)} %all_to_all.22.own_ref), channel_id=1, source_target_pairs={{0,32},{32,0},{64,96},{96,64},{128,160},{160,128},{192,224},{224,1... | collective-permute-start | bytes 1572872 | tf_op jit(solution)/shard_map/ppermute | solution.py:243
  141.9 1.0 convolution_convert_fusion
  143.0 0.5 collective-permute-done.4.other_ref
  143.4 1.1 place.1
  (4 shorter events, 0.1 us)
Async XLA Ops:
  0.6 2.2 %copy-start = (bf16[512,4096]{1,0:T(8,128)(2,1)S(1)}, bf16[512,4096]{1,0:T(8,128)(2,1)}, u32[]{:S(2)}) copy-start(bf16[512,4096]{1,0:T(8,128)(2,1)} %m_ref.3) | copy-start | bytes 12582916
  2.8 1.2 copy-start.2
  4.1 54.5 %copy-start.1 = (bf16[512,4096]{1,0:T(8,128)(2,1)S(1)}, bf16[512,4096]{1,0:T(8,128)(2,1)}, u32[]{:S(2)}) copy-start(bf16[512,4096]{1,0:T(8,128)(2,1)} %m_ref.3) | copy-start | bytes 12582916
  5.8 52.7 %collective-permute-start = (bf16[512,2048]{1,0:T(8,128)(2,1)S(1)}, bf16[512,2048]{1,0:T(8,128)(2,1)S(1)}, u32[]{:S(2)}, u32[]{:S(2)}) collective-permute-start(bf16[512,2048]{1,0:T(8,128)(2,1)S(1)} %get-tuple-element.7), channel_id=1, source_target_pairs={{0,32},{32,0},{64,96},{96,64},{128,160},{160,128},{192,224},{224,1... | collective-permute-start | bytes 6291464 | tf_op jit(solution)/shard_map/ppermute | solution.py:229
  61.2 50.6 %all-to-all-start.2 = ((f32[8,128,256]{2,1,0:T(8,128)}), f32[8,128,256]{2,1,0:T(8,128)S(1)}, u32[]{:S(2)}, u32[]{:S(2)}) async-start(f32[8,128,256]{2,1,0:T(8,128)} %get-tuple-element.9), calls=%async_computation.2 | async-start | bytes 2097152 | tf_op jit(solution)/shard_map/all_to_all | solution.py:235
  68.0 22.9 %collective-permute-start.1 = (f32[128,128]{1,0:T(8,128)S(1)}, f32[128,128]{1,0:T(8,128)S(1)}, u32[]{:S(2)}, u32[]{:S(2)}) collective-permute-start(f32[128,128]{1,0:T(8,128)S(1)} %get-tuple-element.8), channel_id=1, source_target_pairs={{0,64},{32,96},{64,0},{96,32},{128,192},{160,224},{192,128},{224,1... | collective-permute-start | bytes 196616 | tf_op jit(solution)/shard_map/ppermute | solution.py:237
  91.0 7.0 %collective-permute-start.2 = (f32[128,128]{1,0:T(8,128)S(1)}, f32[128,128]{1,0:T(8,128)S(1)}, u32[]{:S(2)}, u32[]{:S(2)}) collective-permute-start(f32[128,128]{1,0:T(8,128)S(1)} %add.18), channel_id=1, source_target_pairs={{0,128},{32,160},{64,192},{96,224},{128,0},{160,32},{192,64},{224,... | collective-permute-start | bytes 196616 | tf_op jit(solution)/shard_map/ppermute | solution.py:237
  98.0 9.5 %collective-permute-start.3 = (f32[128,128]{1,0:T(8,128)S(1)}, f32[128,128]{1,0:T(8,128)S(1)}, u32[]{:S(2)}, u32[]{:S(2)}) collective-permute-start(f32[128,128]{1,0:T(8,128)S(1)} %add.19), channel_id=1, source_target_pairs={{0,256},{32,288},{64,320},{96,352},{128,384},{160,416},{192,448},{... | collective-permute-start | bytes 196616 | tf_op jit(solution)/shard_map/ppermute | solution.py:237
  134.5 8.9 %collective-permute-start.4 = (bf16[8,128,256]{2,1,0:T(8,128)(2,1)S(1)}, bf16[8,128,256]{2,1,0:T(8,128)(2,1)S(1)}, u32[]{:S(2)}, u32[]{:S(2)}) collective-permute-start(bf16[8,128,256]{2,1,0:T(8,128)(2,1)S(1)} %all_to_all.22.own_ref), channel_id=1, source_target_pairs={{0,32},{32,0},{64,96},{96,64},{128,160},{160,128},{192,224},{224,1... | collective-permute-start | bytes 1572872 | tf_op jit(solution)/shard_map/ppermute | solution.py:243

commit v3 on v2

--- a/solution.py
+++ b/solution.py
@@ -27,10 +27,12 @@
     return jnp.broadcast_to(x[:, i : i + 1], (T, K))
 
 
-def chol_inv_kernel(g_ref, o_ref):
+def chol_inv_kernel(z_ref, g_ref, o_ref):
+    z = z_ref[0]
     sub = lax.broadcasted_iota(jnp.int32, (T, K), 0)
     lane = lax.broadcasted_iota(jnp.int32, (T, K), 1)
-    a = [g_ref[p * T : (p + 1) * T, :] for p in range(NP)]
+    per = g_ref.shape[1] // T
+    a = [g_ref[(p // per) ^ z, (p % per) * T : (p % per + 1) * T, :] for p in range(NP)]
     for k in range(NP):
         lo = k * T
         inside = (lane >= lo) & (lane < lo + T)
@@ -59,47 +61,63 @@
         o_ref[lo : lo + T, :] = jnp.where(lane <= lo + sub, u * lax.rsqrt(dvec), 0.0)
 
 
-def chol_inv(gram):
+HBM = pl.BlockSpec(memory_space=pltpu.HBM)
+VMEM = pl.BlockSpec(memory_space=pltpu.VMEM)
+SMEM = pl.BlockSpec(memory_space=pltpu.SMEM)
+STEPS = 8
+
+
+def scalar(value):
+    return value.astype(jnp.int32).reshape(1)
+
+
+def chol_inv(strips, z):
     return pl.pallas_call(
         chol_inv_kernel,
+        in_specs=[SMEM, VMEM],
+        out_specs=VMEM,
         out_shape=jax.ShapeDtypeStruct((K, K), F32),
         compiler_params=room(4),
         name="chol_inv",
-    )(gram)
-
-
-HBM = pl.BlockSpec(memory_space=pltpu.HBM)
-VMEM = pl.BlockSpec(memory_space=pltpu.VMEM)
-SMEM = pl.BlockSpec(memory_space=pltpu.SMEM)
-
-
-def scalar(value):
-    return value.astype(jnp.int32).reshape(1)
-
-
-def sketch_kernel(core_ref, m_ref, o_ref, p_ref, send_ref, sem):
-    half = send_ref.shape[1]
-    at = pl.multiple_of((1 - core_ref[0]) * half, half)
-    copy = pltpu.make_async_copy(m_ref.at[:, pl.ds(at, half)], send_ref, sem)
-    copy.start()
-    p_ref[...] = jnp.dot(m_ref[...], o_ref[...], preferred_element_type=F32)
-    copy.wait()
-
-
-def sketch(matrix, omega, core):
+    )(scalar(z), strips)
+
+
+def sketch_kernel(m_ref, o_ref, p_ref, held, omega, m_sems, o_sems):
+    depth = omega.shape[1]
+    copies = []
+    for k in range(STEPS):
+        cut = pl.ds(k * depth, depth)
+        copies.append(pltpu.make_async_copy(o_ref.at[cut, :], omega.at[k], o_sems.at[k]))
+        copies.append(pltpu.make_async_copy(m_ref.at[:, cut], held.at[k], m_sems.at[k]))
+    for copy in copies:
+        copy.start()
+    for k in range(STEPS):
+        copies[2 * k].wait()
+        copies[2 * k + 1].wait()
+        term = jnp.dot(held[k], omega[k], preferred_element_type=F32)
+        if k == 0:
+            p_ref[...] = term
+        else:
+            p_ref[...] += term
+
+
+def sketch(matrix, omega):
     rows, cols = matrix.shape
+    depth = cols // STEPS
     return pl.pallas_call(
         sketch_kernel,
-        in_specs=[SMEM, VMEM, VMEM],
-        out_specs=[VMEM, VMEM],
-        out_shape=[
-            jax.ShapeDtypeStruct((rows, K), F32),
-            jax.ShapeDtypeStruct((rows, cols // 2), BF16),
+        in_specs=[HBM, HBM],
+        out_specs=VMEM,
+        out_shape=jax.ShapeDtypeStruct((rows, K), F32),
+        scratch_shapes=[
+            pltpu.VMEM((STEPS, rows, depth), BF16),
+            pltpu.VMEM((STEPS, depth, K), BF16),
+            pltpu.SemaphoreType.DMA((STEPS,)),
+            pltpu.SemaphoreType.DMA((STEPS,)),
         ],
-        scratch_shapes=[pltpu.SemaphoreType.DMA],
-        compiler_params=room(16),
+        compiler_params=room(56),
         name="sketch",
-    )(scalar(core), matrix, omega)
+    )(matrix, omega)
 
 
 def share_kernel(parts_ref, out_ref):
@@ -117,45 +135,58 @@
         out_specs=VMEM,
         out_shape=jax.ShapeDtypeStruct((copies, *parts.shape[1:]), F32),
         compiler_params=room(4),
+        cost_estimate=pl.CostEstimate(flops=2_500_000_000, bytes_accessed=8 << 20, transcendentals=0),
         name="share",
     )(parts)
 
 
-def w_kernel(core_ref, s_ref, m_ref, his_ref, gram_ref, w_ref):
-    rows, half = his_ref.shape
-    width = w_ref.shape[2]
-    both = s_ref[...]
-    gram_ref[...] = lax.dot_general(
-        both, both, (((0,), (0,)), ((), ())), precision=HIGH, preferred_element_type=F32
+def gram_kernel(z_ref, s_ref, out_ref, held):
+    held[...] = lax.dot_general(
+        s_ref[...], s_ref[...], (((0,), (0,)), ((), ())), precision=HIGH, preferred_element_type=F32
     )
+    tall = out_ref.shape[1]
+    strip = held[pl.ds(pl.multiple_of(z_ref[0] * tall, tall), tall), :]
+    for k in range(NROW):
+        out_ref[k] = strip
+
+
+def gram_strips(sampled, z):
+    return pl.pallas_call(
+        gram_kernel,
+        in_specs=[SMEM, VMEM],
+        out_specs=VMEM,
+        out_shape=jax.ShapeDtypeStruct((NROW, K // NZ, K), F32),
+        scratch_shapes=[pltpu.VMEM((K, K), F32)],
+        compiler_params=room(8),
+        cost_estimate=pl.CostEstimate(flops=2_500_000_000, bytes_accessed=8 << 20, transcendentals=0),
+        name="gram_strips",
+    )(scalar(z), sampled)
+
+
+def w_kernel(core_ref, s_ref, m_ref, own_ref, other_ref):
+    turned = s_ref[...].T
+    high = turned.astype(BF16)
+    low = (turned - high.astype(F32)).astype(BF16)
+    hl = jnp.concatenate([high, low], axis=0)
+    width = own_ref.shape[2]
     core = core_ref[0]
-    terms = []
-    for who in (core, 1 - core):
-        turned = s_ref[pl.ds(pl.multiple_of(who * rows, rows), rows), :].T
-        high = turned.astype(BF16)
-        low = (turned - high.astype(F32)).astype(BF16)
-        terms.append(jnp.concatenate([high, low], axis=0))
-    for y in range(NY):
-        at = pl.multiple_of(core * half + y * width, width)
-        w = jnp.dot(terms[0], m_ref[:, pl.ds(at, width)], preferred_element_type=F32)
-        cut = slice(y * width, (y + 1) * width)
-        w = w + jnp.dot(terms[1], his_ref[:, cut], preferred_element_type=F32)
-        w_ref[y] = w[:K] + w[K:]
-
-
-def sketch_rows(both, matrix, his, core):
-    width = his.shape[1] // NY
+    for half, out_ref in ((1 - core, other_ref), (core, own_ref)):
+        for y in range(NY):
+            at = pl.multiple_of((half * NY + y) * width, width)
+            w = jnp.dot(hl, m_ref[:, pl.ds(at, width)], preferred_element_type=F32)
+            out_ref[y] = w[:K] + w[K:]
+
+
+def sketch_rows(sampled, matrix, core):
+    width = matrix.shape[1] // NROW
     return pl.pallas_call(
         w_kernel,
-        in_specs=[SMEM, VMEM, VMEM, VMEM],
+        in_specs=[SMEM, VMEM, VMEM],
         out_specs=[VMEM, VMEM],
-        out_shape=[
-            jax.ShapeDtypeStruct((K, K), F32),
-            jax.ShapeDtypeStruct((NY, K, width), F32),
-        ],
+        out_shape=[jax.ShapeDtypeStruct((NY, K, width), F32)] * 2,
         compiler_params=room(20),
         name="sketch_rows",
-    )(scalar(core), both, matrix, his)
+    )(scalar(core), sampled, matrix)
 
 
 def finish_kernel(inv_ref, parts_ref, out_ref, held, sems):
@@ -215,30 +246,29 @@
 
 SWAP = [(i, i ^ 1) for i in range(NROW)]
 Y_GROUPS = [[2 * k + core for k in range(NY)] for core in range(2)]
-CHIP_GROUPS = [
-    [(2 * y + core) * NCOL + c for core in range(2) for c in range(NCOL)] for y in range(NY)
-]
 
 
 def local(matrix, omega):
     core = lax.axis_index("row") % 2
+    z = lax.axis_index("col") % NZ
     rows = matrix.shape[0]
 
-    partial_value, send = sketch(matrix, omega, core)
+    partial_value = sketch(matrix, omega)
     parts = lax.all_to_all(partial_value.reshape(NCOL, rows // NCOL, K), "col", 0, 0)
-    his = lax.ppermute(send, "row", SWAP)
-    both = lax.all_to_all(
-        share(parts, 2 * NCOL), ("row", "col"), 0, 0, axis_index_groups=CHIP_GROUPS
-    ).reshape(2 * rows, K)
-
-    gram, w = sketch_rows(both, matrix, his, core)
-    parts = lax.all_to_all(w, "row", 0, 0, axis_index_groups=Y_GROUPS)
+    sampled = lax.all_to_all(share(parts, NCOL), "col", 0, 0).reshape(rows, K)
+
+    strips = gram_strips(sampled, z)
+    held, strips = lax.optimization_barrier((sampled, strips))
+    strips = share(lax.all_to_all(strips, "row", 0, 0), 1)
+    own, other = sketch_rows(held, matrix, core)
+    mine = own + lax.ppermute(other, "row", SWAP)
+    parts = lax.all_to_all(mine, "row", 0, 0, axis_index_groups=Y_GROUPS)
     for step in (1, 2, 4):
-        gram = gram + lax.ppermute(gram, "row", [(i, i ^ (2 * step)) for i in range(NROW)])
-    inverse = chol_inv(gram)
+        theirs = lax.ppermute(strips, "col", [(i, i ^ step) for i in range(NCOL)])
+        strips = jnp.concatenate([strips, theirs], axis=0)
+    inverse = chol_inv(strips, z)
 
     pieces = lax.all_to_all(finish(inverse, parts), "row", 0, 0, axis_index_groups=Y_GROUPS)
-    sampled = lax.dynamic_slice_in_dim(both, core * rows, rows, 0)
     basis = lax.dot_general(sampled, inverse, (((1,), (1,)), ((), ())), precision=HIGH).astype(BF16)
     return basis, place(pieces, lax.ppermute(pieces, "row", SWAP), core)
 

time: 145 us -> 131 us (0.903)
  blocking collectives: 64.8 us -> 41.5 us
  waiting for transfers between devices: 23.7 us -> 32.3 us
  Pallas kernels: 11.7 us -> 14.9 us
  local copies, waits for them, and re-layouts: 3.41 us -> 1.15 us
    all_to_all x1 -> x0, blocking collectives: 26.2 us -> none  [local(): lax.all_to_all(share(parts, 2 * NCOL), ('row', 'col'), 0, 0, axis_index_g...]
    all_to_all x1 -> x3, waiting for transfers between devices: 0.01 us -> 23.6 us  [the longest x1 9.64 us: local(): sampled = lax.all_to_all(share(parts, NCOL), 'col', 0, 0).reshape(rows, K)]
    ppermute x4, waiting for transfers between devices: 23.3 us -> 8.28 us  [the longest x3 8.28 us: local(): theirs = lax.ppermute(strips, 'col', [(i, i ^ step) for i in range(NCOL)])]
    all_to_all x1 -> x3, starting transfers between devices: 6.82 us -> 17.1 us  [the longest x1 7.24 us: local(): strips = share(lax.all_to_all(strips, 'row', 0, 0), 1)]
    ppermute x4, starting transfers between devices: 24.9 us -> 16.2 us  [the longest x3 10.7 us: local(): theirs = lax.ppermute(strips, 'col', [(i, i ^ step) for i in range(NCOL)])]
    all_to_all x1, blocking collectives: 17.6 us -> 23.4 us  [local(): lax.all_to_all(partial_value.reshape(NCOL, rows // NCOL, K), 'col', 0, 0)]
    all_to_all x1, blocking collectives: 20.9 us -> 18.1 us  [local(): lax.all_to_all(finish(inverse, parts), 'row', 0, 0, axis_index_groups=Y_G...]
    ppermute x1, starting transfers between devices: 7.37 us -> 4.66 us  [local(): return (basis, place(pieces, lax.ppermute(pieces, 'row', SWAP), core))]
  transfers between devices with their start and end apart: 6 -> 8, of which waited for: 4 -> 7; matrix products, arithmetic and copies ran while one was open for 1% -> 2% of each run, Pallas kernels for 3% -> 3%
where the time goes in v3:
time: 131 us
  blocking collectives  41.5 us (32%)
  starting transfers between devices  37.9 us (29%)
  waiting for transfers between devices  32.3 us (25%)
  Pallas kernels  14.9 us (11%)
    all_to_all x1, blocking collectives, local(): lax.all_to_all(partial_value.reshape(NCOL, rows // NCOL, K), 'col', 0, 0)  23.4 us
    all_to_all x1, blocking collectives, local(): lax.all_to_all(finish(inverse, parts), 'row', 0, 0, axis_index_groups=Y_G...  18.1 us
    ppermute x3, starting transfers between devices, local(): theirs = lax.ppermute(strips, 'col', [(i, i ^ step) for i in range(NCOL)])  10.7 us
    all_to_all x1, waiting for transfers between devices, local(): sampled = lax.all_to_all(share(parts, NCOL), 'col', 0, 0).reshape(rows, K)  9.64 us
    ppermute x3, waiting for transfers between devices, local(): theirs = lax.ppermute(strips, 'col', [(i, i ^ step) for i in range(NCOL)])  8.28 us
    all_to_all x1, waiting for transfers between devices, local(): strips = share(lax.all_to_all(strips, 'row', 0, 0), 1)  8.02 us
    all_to_all x1, starting transfers between devices, local(): strips = share(lax.all_to_all(strips, 'row', 0, 0), 1)  7.24 us
    all_to_all x1, starting transfers between devices, local(): sampled = lax.all_to_all(share(parts, NCOL), 'col', 0, 0).reshape(rows, K)  6.29 us
  transfers between devices with their start and end apart: 8, of which 7 were waited for; matrix products, arithmetic and copies ran while one was open for 2% of the time, Pallas kernels for 3%

profile of v3, /device:TPU:1, one launch (start us, length us, event | category | flops | bytes accessed | tf_op | source)
XLA Modules:
  0.0 130.8 jit_solution(14577040091809604757)
XLA Ops:
  0.6 4.6 %sketch.1 = f32[512,128]{1,0:T(8,128)} custom-call(bf16[512,4096]{1,0:T(8,128)(2,1)} %m_ref.3, bf16[4096,128]{1,0:T(8,128)(2,1)} %o_ref.1), custom_call_target="tpu_custom_call" | custom-call | tf_op jit(solution)/shard_map/sketch/pallas_call | solution.py:107
  5.3 23.4 %all_to_all.25.parts_ref = f32[32,16,128]{2,1,0:T(8,128)S(1)} all-to-all(f32[32,16,128]{2,1,0:T(8,128)} %bitcast.9), channel_id=1, replica_groups=mesh['row'=16,'col'=32] {'col'}, dimensions={0} | all-to-all | bytes 524288 | tf_op jit(solution)/shard_map/all_to_all | solution.py:257
  28.7 0.7 share.2
  29.4 6.3 %all-to-all-start.1 = ((f32[32,16,128]{2,1,0:T(8,128)}), f32[32,16,128]{2,1,0:T(8,128)S(1)}, u32[]{:S(2)}, u32[]{:S(2)}) async-start(f32[32,16,128]{2,1,0:T(8,128)} %share.2), calls=%async_computation.1 | async-start | bytes 524288 | tf_op jit(solution)/shard_map/all_to_all | solution.py:258
  35.7 9.6 %all-to-all-done.1 = f32[32,16,128]{2,1,0:T(8,128)S(1)} async-done(((f32[32,16,128]{2,1,0:T(8,128)}), f32[32,16,128]{2,1,0:T(8,128)S(1)}, u32[]{:S(2)}, u32[]{:S(2)}) %all-to-all-start.1) | async-done | bytes 262176 | tf_op jit(solution)/shard_map/all_to_all | solution.py:258
  45.4 0.0 copy-start
  45.4 1.1 gram_strips.1
  46.5 1.1 copy-done
  47.6 1.3 sketch_rows.1
  48.9 5.5 %collective-permute-start.3 = (f32[8,128,256]{2,1,0:T(8,128)S(1)}, f32[8,128,256]{2,1,0:T(8,128)S(1)}, u32[]{:S(2)}, u32[]{:S(2)}) collective-permute-start(f32[8,128,256]{2,1,0:T(8,128)S(1)} %get-tuple-element.9), channel_id=1, source_target_pairs={{0,32},{32,0},{64,96},{96,64},{128,160},{160,128},{192,224},{224,1... | collective-permute-start | bytes 3145736 | tf_op jit(solution)/shard_map/ppermute | solution.py:264
  54.4 7.2 %all-to-all-start.2 = ((f32[16,16,128]{2,1,0:T(8,128)}), f32[16,16,128]{2,1,0:T(8,128)S(1)}, u32[]{:S(2)}, u32[]{:S(2)}) async-start(f32[16,16,128]{2,1,0:T(8,128)} %gram_strips.1), calls=%async_computation.2 | async-start | bytes 262144 | tf_op jit(solution)/shard_map/all_to_all | solution.py:262
  61.7 0.0 collective-permute-done.3
  61.7 1.1 add.12
  62.8 8.0 %all-to-all-done.2.parts_ref = f32[16,16,128]{2,1,0:T(8,128)S(1)} async-done(((f32[16,16,128]{2,1,0:T(8,128)}), f32[16,16,128]{2,1,0:T(8,128)S(1)}, u32[]{:S(2)}, u32[]{:S(2)}) %all-to-all-start.2) | async-done | bytes 131104 | tf_op jit(solution)/shard_map/all_to_all | solution.py:262
  70.8 3.6 %all-to-all-start.3 = ((f32[8,128,256]{2,1,0:T(8,128)}), f32[8,128,256]{2,1,0:T(8,128)S(1)}, u32[]{:S(2)}, u32[]{:S(2)}) async-start(f32[8,128,256]{2,1,0:T(8,128)} %add.12), calls=%async_computation.3 | async-start | bytes 2097152 | tf_op jit(solution)/shard_map/all_to_all | solution.py:265
  74.4 3.4 %collective-permute-start = (f32[1,16,128]{2,1,0:T(8,128)S(1)}, f32[1,16,128]{2,1,0:T(8,128)S(1)}, u32[]{:S(2)}, u32[]{:S(2)}) collective-permute-start(f32[1,16,128]{2,1,0:T(8,128)S(1)} %share.3), channel_id=1, source_target_pairs={{0,1},{1,0},{2,3},{3,2},{4,5},{5,4},{6,7},{7,6},{8,9},{9,8},{10,11... | collective-permute-start | bytes 24584 | tf_op jit(solution)/shard_map/ppermute | solution.py:267
  77.8 1.3 %collective-permute-done = f32[1,16,128]{2,1,0:T(8,128)S(1)} collective-permute-done((f32[1,16,128]{2,1,0:T(8,128)S(1)}, f32[1,16,128]{2,1,0:T(8,128)S(1)}, u32[]{:S(2)}, u32[]{:S(2)}) %collective-permute-start) | collective-permute-done | bytes 8224 | tf_op jit(solution)/shard_map/ppermute | solution.py:267
  79.2 3.7 %collective-permute-start.1 = (f32[2,16,128]{2,1,0:T(8,128)S(1)}, f32[2,16,128]{2,1,0:T(8,128)S(1)}, u32[]{:S(2)}, u32[]{:S(2)}) collective-permute-start(f32[2,16,128]{2,1,0:T(8,128)S(1)} %pad_maximum_fusion.2), channel_id=1, source_target_pairs={{0,2},{1,3},{2,0},{3,1},{4,6},{5,7},{6,4},{7,5},{8,10},{9,11},{10,... | collective-permute-start | bytes 49160 | tf_op jit(solution)/shard_map/ppermute | solution.py:267
  82.8 2.0 %collective-permute-done.1 = f32[2,16,128]{2,1,0:T(8,128)S(1)} collective-permute-done((f32[2,16,128]{2,1,0:T(8,128)S(1)}, f32[2,16,128]{2,1,0:T(8,128)S(1)}, u32[]{:S(2)}, u32[]{:S(2)}) %collective-permute-start.1) | collective-permute-done | bytes 16416 | tf_op jit(solution)/shard_map/ppermute | solution.py:267
  84.8 3.6 %collective-permute-start.2 = (f32[4,16,128]{2,1,0:T(8,128)S(1)}, f32[4,16,128]{2,1,0:T(8,128)S(1)}, u32[]{:S(2)}, u32[]{:S(2)}) collective-permute-start(f32[4,16,128]{2,1,0:T(8,128)S(1)} %pad_maximum_fusion.1), channel_id=1, source_target_pairs={{0,4},{1,5},{2,6},{3,7},{4,0},{5,1},{6,2},{7,3},{8,12},{9,13},{10,... | collective-permute-start | bytes 98312 | tf_op jit(solution)/shard_map/ppermute | solution.py:267
  88.5 5.0 %collective-permute-done.2 = f32[4,16,128]{2,1,0:T(8,128)S(1)} collective-permute-done((f32[4,16,128]{2,1,0:T(8,128)S(1)}, f32[4,16,128]{2,1,0:T(8,128)S(1)}, u32[]{:S(2)}, u32[]{:S(2)}) %collective-permute-start.2) | collective-permute-done | bytes 32800 | tf_op jit(solution)/shard_map/ppermute | solution.py:267
  93.4 4.3 %chol_inv.1.inv_ref = f32[128,128]{1,0:T(8,128)S(1)} custom-call(s32[1]{0:T(128)} %bitcast.2.z_ref, f32[8,16,128]{2,1,0:T(8,128)S(1)} %pad_maximum_fusion.g_ref), custom_call_target="tpu_custom_call" | custom-call | tf_op jit(solution)/shard_map/chol_inv/pallas_call | solution.py:75
  97.8 5.9 %all-to-all-done.3.parts_ref = f32[8,128,256]{2,1,0:T(8,128)S(1)} async-done(((f32[8,128,256]{2,1,0:T(8,128)}), f32[8,128,256]{2,1,0:T(8,128)S(1)}, u32[]{:S(2)}, u32[]{:S(2)}) %all-to-all-start.3) | async-done | bytes 1048608 | tf_op jit(solution)/shard_map/all_to_all | solution.py:265
  103.7 1.7 %finish.1 = bf16[8,128,256]{2,1,0:T(8,128)(2,1)S(1)} custom-call(f32[128,128]{1,0:T(8,128)S(1)} %chol_inv.1.inv_ref, f32[8,128,256]{2,1,0:T(8,128)S(1)} %all-to-all-done.3.parts_ref), custom_call_target="tpu_custom_call" | custom-call | tf_op jit(solution)/shard_map/finish/pallas_call | solution.py:207
  105.4 18.1 %all_to_all.26.own_ref = bf16[8,128,256]{2,1,0:T(8,128)(2,1)S(1)} all-to-all(bf16[8,128,256]{2,1,0:T(8,128)(2,1)S(1)} %finish.1), channel_id=1, replica_groups={{0,64,128,192,256,320,384,448},{32,96,160,224,288,352,416,480},{1,65,12..., dimensions={0} | all-to-all | bytes 1048576 | tf_op jit(solution)/shard_map/all_to_all | solution.py:271
  123.5 4.7 %collective-permute-start.4 = (bf16[8,128,256]{2,1,0:T(8,128)(2,1)S(1)}, bf16[8,128,256]{2,1,0:T(8,128)(2,1)S(1)}, u32[]{:S(2)}, u32[]{:S(2)}) collective-permute-start(bf16[8,128,256]{2,1,0:T(8,128)(2,1)S(1)} %all_to_all.26.own_ref), channel_id=1, source_target_pairs={{0,32},{32,0},{64,96},{96,64},{128,160},{160,128},{192,224},{224,1... | collective-permute-start | bytes 1572872 | tf_op jit(solution)/shard_map/ppermute | solution.py:273
  128.2 1.0 convolution_convert_fusion
  129.2 0.5 collective-permute-done.4.other_ref
  129.7 1.1 place.1
  (4 shorter events, 0.0 us)
Async XLA Ops:
  29.4 16.0 %all-to-all-start.1 = ((f32[32,16,128]{2,1,0:T(8,128)}), f32[32,16,128]{2,1,0:T(8,128)S(1)}, u32[]{:S(2)}, u32[]{:S(2)}) async-start(f32[32,16,128]{2,1,0:T(8,128)} %share.2), calls=%async_computation.1 | async-start | bytes 524288 | tf_op jit(solution)/shard_map/all_to_all | solution.py:258
  45.4 2.2 %copy-start = (bf16[512,4096]{1,0:T(8,128)(2,1)S(1)}, bf16[512,4096]{1,0:T(8,128)(2,1)}, u32[]{:S(2)}) copy-start(bf16[512,4096]{1,0:T(8,128)(2,1)} %m_ref.3) | copy-start | bytes 12582916
  48.9 12.8 %collective-permute-start.3 = (f32[8,128,256]{2,1,0:T(8,128)S(1)}, f32[8,128,256]{2,1,0:T(8,128)S(1)}, u32[]{:S(2)}, u32[]{:S(2)}) collective-permute-start(f32[8,128,256]{2,1,0:T(8,128)S(1)} %get-tuple-element.9), channel_id=1, source_target_pairs={{0,32},{32,0},{64,96},{96,64},{128,160},{160,128},{192,224},{224,1... | collective-permute-start | bytes 3145736 | tf_op jit(solution)/shard_map/ppermute | solution.py:264
  54.4 16.4 %all-to-all-start.2 = ((f32[16,16,128]{2,1,0:T(8,128)}), f32[16,16,128]{2,1,0:T(8,128)S(1)}, u32[]{:S(2)}, u32[]{:S(2)}) async-start(f32[16,16,128]{2,1,0:T(8,128)} %gram_strips.1), calls=%async_computation.2 | async-start | bytes 262144 | tf_op jit(solution)/shard_map/all_to_all | solution.py:262
  70.8 32.8 %all-to-all-start.3 = ((f32[8,128,256]{2,1,0:T(8,128)}), f32[8,128,256]{2,1,0:T(8,128)S(1)}, u32[]{:S(2)}, u32[]{:S(2)}) async-start(f32[8,128,256]{2,1,0:T(8,128)} %add.12), calls=%async_computation.3 | async-start | bytes 2097152 | tf_op jit(solution)/shard_map/all_to_all | solution.py:265
  74.4 4.7 %collective-permute-start = (f32[1,16,128]{2,1,0:T(8,128)S(1)}, f32[1,16,128]{2,1,0:T(8,128)S(1)}, u32[]{:S(2)}, u32[]{:S(2)}) collective-permute-start(f32[1,16,128]{2,1,0:T(8,128)S(1)} %share.3), channel_id=1, source_target_pairs={{0,1},{1,0},{2,3},{3,2},{4,5},{5,4},{6,7},{7,6},{8,9},{9,8},{10,11... | collective-permute-start | bytes 24584 | tf_op jit(solution)/shard_map/ppermute | solution.py:267
  79.2 5.7 %collective-permute-start.1 = (f32[2,16,128]{2,1,0:T(8,128)S(1)}, f32[2,16,128]{2,1,0:T(8,128)S(1)}, u32[]{:S(2)}, u32[]{:S(2)}) collective-permute-start(f32[2,16,128]{2,1,0:T(8,128)S(1)} %pad_maximum_fusion.2), channel_id=1, source_target_pairs={{0,2},{1,3},{2,0},{3,1},{4,6},{5,7},{6,4},{7,5},{8,10},{9,11},{10,... | collective-permute-start | bytes 49160 | tf_op jit(solution)/shard_map/ppermute | solution.py:267
  84.8 8.6 %collective-permute-start.2 = (f32[4,16,128]{2,1,0:T(8,128)S(1)}, f32[4,16,128]{2,1,0:T(8,128)S(1)}, u32[]{:S(2)}, u32[]{:S(2)}) collective-permute-start(f32[4,16,128]{2,1,0:T(8,128)S(1)} %pad_maximum_fusion.1), channel_id=1, source_target_pairs={{0,4},{1,5},{2,6},{3,7},{4,0},{5,1},{6,2},{7,3},{8,12},{9,13},{10,... | collective-permute-start | bytes 98312 | tf_op jit(solution)/shard_map/ppermute | solution.py:267
  123.5 6.2 %collective-permute-start.4 = (bf16[8,128,256]{2,1,0:T(8,128)(2,1)S(1)}, bf16[8,128,256]{2,1,0:T(8,128)(2,1)S(1)}, u32[]{:S(2)}, u32[]{:S(2)}) collective-permute-start(bf16[8,128,256]{2,1,0:T(8,128)(2,1)S(1)} %all_to_all.26.own_ref), channel_id=1, source_target_pairs={{0,32},{32,0},{64,96},{96,64},{128,160},{160,128},{192,224},{224,1... | collective-permute-start | bytes 1572872 | tf_op jit(solution)/shard_map/ppermute | solution.py:273

commit v4 on v3

--- a/solution.py
+++ b/solution.py
@@ -27,12 +27,16 @@
     return jnp.broadcast_to(x[:, i : i + 1], (T, K))
 
 
-def chol_inv_kernel(z_ref, g_ref, o_ref):
+def chol_inv_kernel(z_ref, g_ref, o_ref, q_ref):
     z = z_ref[0]
     sub = lax.broadcasted_iota(jnp.int32, (T, K), 0)
     lane = lax.broadcasted_iota(jnp.int32, (T, K), 1)
     per = g_ref.shape[1] // T
     a = [g_ref[(p // per) ^ z, (p % per) * T : (p % per + 1) * T, :] for p in range(NP)]
+    squares = jnp.zeros((T, K), F32)
+    diagonal = jnp.zeros((T, K), F32)
+    for p in range(NP):
+        diagonal = jnp.where(lane == p * T + sub, a[p], diagonal)
     for k in range(NP):
         lo = k * T
         inside = (lane >= lo) & (lane < lo + T)
@@ -58,13 +62,17 @@
             while len(terms) > 1:
                 terms = [terms[i] + terms[i + 1] for i in range(0, len(terms), 2)]
             a[p] = jnp.where(inside, 0.0, a[p]) - terms[0]
-        o_ref[lo : lo + T, :] = jnp.where(lane <= lo + sub, u * lax.rsqrt(dvec), 0.0)
+        done = jnp.where(lane <= lo + sub, u * lax.rsqrt(dvec), 0.0)
+        o_ref[lo : lo + T, :] = done
+        squares = squares + done * done
+    q_ref[...] = squares * jnp.sum(diagonal, axis=0, keepdims=True)
 
 
 HBM = pl.BlockSpec(memory_space=pltpu.HBM)
 VMEM = pl.BlockSpec(memory_space=pltpu.VMEM)
 SMEM = pl.BlockSpec(memory_space=pltpu.SMEM)
-STEPS = 8
+STEPS = 4
+STRIPS = 4
 
 
 def scalar(value):
@@ -75,8 +83,8 @@
     return pl.pallas_call(
         chol_inv_kernel,
         in_specs=[SMEM, VMEM],
-        out_specs=VMEM,
-        out_shape=jax.ShapeDtypeStruct((K, K), F32),
+        out_specs=[VMEM, VMEM],
+        out_shape=[jax.ShapeDtypeStruct((K, K), F32), jax.ShapeDtypeStruct((T, K), F32)],
         compiler_params=room(4),
         name="chol_inv",
     )(scalar(z), strips)
@@ -155,7 +163,7 @@
         gram_kernel,
         in_specs=[SMEM, VMEM],
         out_specs=VMEM,
-        out_shape=jax.ShapeDtypeStruct((NROW, K // NZ, K), F32),
+        out_shape=jax.ShapeDtypeStruct((NROW, K // STRIPS, K), F32),
         scratch_shapes=[pltpu.VMEM((K, K), F32)],
         compiler_params=room(8),
         cost_estimate=pl.CostEstimate(flops=2_500_000_000, bytes_accessed=8 << 20, transcendentals=0),
@@ -189,30 +197,44 @@
     )(scalar(core), sampled, matrix)
 
 
-def finish_kernel(inv_ref, parts_ref, out_ref, held, sems):
-    copies = [pltpu.make_async_copy(parts_ref.at[k], held.at[k], sems.at[k]) for k in range(NY)]
-    for copy in copies:
-        copy.start()
-    copies[0].wait()
-    total = held[0]
-    for k in range(1, NY):
-        copies[k].wait()
-        total = total + held[k]
-    piece = jnp.dot(inv_ref[...], total, precision=HIGH, preferred_element_type=F32).astype(BF16)
+def fold_kernel(a_ref, b_ref, high_ref, low_ref):
+    for y in range(NY):
+        w = a_ref[y] + b_ref[y]
+        high = w.astype(BF16)
+        high_ref[y] = high
+        low_ref[y] = (w - high.astype(F32)).astype(BF16)
+
+
+def fold(a, b):
+    return pl.pallas_call(
+        fold_kernel,
+        in_specs=[VMEM, VMEM],
+        out_specs=[VMEM, VMEM],
+        out_shape=[jax.ShapeDtypeStruct(a.shape, BF16)] * 2,
+        compiler_params=room(8),
+        name="fold",
+    )(a, b)
+
+
+def finish_kernel(inv_ref, *refs):
+    out_ref = refs[-1]
+    terms = [ref[k].astype(F32) for ref in refs[:-1] for k in range(NY)]
+    while len(terms) > 1:
+        terms = [terms[i] + terms[i + 1] for i in range(0, len(terms), 2)]
+    piece = jnp.dot(inv_ref[...], terms[0], precision=HIGH, preferred_element_type=F32).astype(BF16)
     for k in range(NY):
         out_ref[k] = piece
 
 
-def finish(inverse, parts):
+def finish(inverse, *parts):
     return pl.pallas_call(
         finish_kernel,
-        in_specs=[VMEM, pl.BlockSpec(memory_space=pl.ANY)],
+        in_specs=[VMEM] * (1 + len(parts)),
         out_specs=VMEM,
-        out_shape=jax.ShapeDtypeStruct(parts.shape, BF16),
-        scratch_shapes=[pltpu.VMEM(parts.shape, F32), pltpu.SemaphoreType.DMA((NY,))],
+        out_shape=jax.ShapeDtypeStruct(parts[0].shape, BF16),
         compiler_params=room(8),
         name="finish",
-    )(inverse, parts)
+    )(inverse, *parts)
 
 
 def place_kernel(core_ref, own_ref, other_ref, out_ref, sems):
@@ -248,9 +270,13 @@
 Y_GROUPS = [[2 * k + core for k in range(NY)] for core in range(2)]
 
 
+def over_y(blocks):
+    return lax.all_to_all(blocks, "row", 0, 0, axis_index_groups=Y_GROUPS)
+
+
 def local(matrix, omega):
     core = lax.axis_index("row") % 2
-    z = lax.axis_index("col") % NZ
+    z = lax.axis_index("col") % NZ // 2
     rows = matrix.shape[0]
 
     partial_value = sketch(matrix, omega)
@@ -261,14 +287,19 @@
     held, strips = lax.optimization_barrier((sampled, strips))
     strips = share(lax.all_to_all(strips, "row", 0, 0), 1)
     own, other = sketch_rows(held, matrix, core)
-    mine = own + lax.ppermute(other, "row", SWAP)
-    parts = lax.all_to_all(mine, "row", 0, 0, axis_index_groups=Y_GROUPS)
-    for step in (1, 2, 4):
+    high, low = fold(own, lax.ppermute(other, "row", SWAP))
+    parts = over_y(high)
+    for step in (2, 4):
         theirs = lax.ppermute(strips, "col", [(i, i ^ step) for i in range(NCOL)])
         strips = jnp.concatenate([strips, theirs], axis=0)
-    inverse = chol_inv(strips, z)
-
-    pieces = lax.all_to_all(finish(inverse, parts), "row", 0, 0, axis_index_groups=Y_GROUPS)
+    inverse, growth = chol_inv(strips, z)
+
+    pieces = lax.cond(
+        jnp.sum(growth) <= 2.0 * K,
+        lambda: finish(inverse, parts),
+        lambda: finish(inverse, parts, over_y(low)),
+    )
+    pieces = over_y(pieces)
     basis = lax.dot_general(sampled, inverse, (((1,), (1,)), ((), ())), precision=HIGH).astype(BF16)
     return basis, place(pieces, lax.ppermute(pieces, "row", SWAP), core)
 

time: 131 us -> 128 us (0.977)
  waiting for transfers between devices: 32.3 us -> 27.6 us
  blocking collectives: 41.5 us -> 44.1 us
  starting transfers between devices: 37.9 us -> 36.1 us
    all_to_all x1, waiting for transfers between devices: 5.92 us -> 0.01 us  [over_y(): return lax.all_to_all(blocks, 'row', 0, 0, axis_index_groups=Y_GROUPS)]
    ppermute x3 -> x2, starting transfers between devices: 10.7 us -> 7.71 us  [local(): theirs = lax.ppermute(strips, 'col', [(i, i ^ step) for i in range(NCOL)])]
    all_to_all x1, waiting for transfers between devices: 8.02 us -> 10.8 us  [local(): strips = share(lax.all_to_all(strips, 'row', 0, 0), 1)]
    all_to_all x1, blocking collectives: 18.1 us -> 20.7 us  [over_y(): return lax.all_to_all(blocks, 'row', 0, 0, axis_index_groups=Y_GROUPS)]
    ppermute x3 -> x2, waiting for transfers between devices: 8.28 us -> 6.72 us  [local(): theirs = lax.ppermute(strips, 'col', [(i, i ^ step) for i in range(NCOL)])]
    pallas_call x2 -> x3, Pallas kernels: 6.04 us -> 5.55 us  [the longest x1 4.31 us: chol_inv(): pl.pallas_call(chol_inv_kernel, in_specs=[SMEM, VMEM], out_specs=[VMEM, V...]
  transfers between devices with their start and end apart: 8 -> 7, of which waited for: 7 -> 5; matrix products, arithmetic and copies ran while one was open for 2% -> 1% of each run, Pallas kernels for 3% -> 4%
where the time goes in v4:
time: 128 us; the launch traced here: 127 us
  blocking collectives  44.1 us (34%)
  starting transfers between devices  36.1 us (28%)
  waiting for transfers between devices  27.6 us (22%)
  Pallas kernels  14.9 us (12%)
  between operations  1.42 us (1%)
    all_to_all x1, blocking collectives, local(): lax.all_to_all(partial_value.reshape(NCOL, rows // NCOL, K), 'col', 0, 0)  23.4 us
    all_to_all x1, blocking collectives, over_y(): return lax.all_to_all(blocks, 'row', 0, 0, axis_index_groups=Y_GROUPS)  20.7 us
    all_to_all x1, waiting for transfers between devices, local(): strips = share(lax.all_to_all(strips, 'row', 0, 0), 1)  10.8 us
    all_to_all x1, waiting for transfers between devices, local(): sampled = lax.all_to_all(share(parts, NCOL), 'col', 0, 0).reshape(rows, K)  9.62 us
    ppermute x2, starting transfers between devices, local(): theirs = lax.ppermute(strips, 'col', [(i, i ^ step) for i in range(NCOL)])  7.71 us
    all_to_all x1, starting transfers between devices, local(): strips = share(lax.all_to_all(strips, 'row', 0, 0), 1)  7.24 us
    ppermute x2, waiting for transfers between devices, local(): theirs = lax.ppermute(strips, 'col', [(i, i ^ step) for i in range(NCOL)])  6.72 us
    all_to_all x1, starting transfers between devices, local(): sampled = lax.all_to_all(share(parts, NCOL), 'col', 0, 0).reshape(rows, K)  6.29 us
  transfers between devices with their start and end apart: 7, of which 5 were waited for; matrix products, arithmetic and copies ran while one was open for 1% of the time, Pallas kernels for 4%

profile of v4, /device:TPU:1, one launch (start us, length us, event | category | flops | bytes accessed | tf_op | source)
XLA Modules:
  0.0 127.0 jit_solution(14173202523057032252)
XLA Ops:
  0.6 4.6 %sketch.1 = f32[512,128]{1,0:T(8,128)} custom-call(bf16[512,4096]{1,0:T(8,128)(2,1)} %m_ref.3, bf16[4096,128]{1,0:T(8,128)(2,1)} %o_ref.1), custom_call_target="tpu_custom_call" | custom-call | tf_op jit(solution)/shard_map/sketch/pallas_call | solution.py:115
  5.3 23.4 %all_to_all.30.parts_ref = f32[32,16,128]{2,1,0:T(8,128)S(1)} all-to-all(f32[32,16,128]{2,1,0:T(8,128)} %bitcast.9), channel_id=1, replica_groups=mesh['row'=16,'col'=32] {'col'}, dimensions={0} | all-to-all | bytes 524288 | tf_op jit(solution)/shard_map/all_to_all | solution.py:283
  28.7 0.7 share.2
  29.4 6.3 %all-to-all-start.2 = ((f32[32,16,128]{2,1,0:T(8,128)}), f32[32,16,128]{2,1,0:T(8,128)S(1)}, u32[]{:S(2)}, u32[]{:S(2)}) async-start(f32[32,16,128]{2,1,0:T(8,128)} %share.2), calls=%async_computation.2 | async-start | bytes 524288 | tf_op jit(solution)/shard_map/all_to_all | solution.py:284
  35.7 9.6 %all-to-all-done.2 = f32[32,16,128]{2,1,0:T(8,128)S(1)} async-done(((f32[32,16,128]{2,1,0:T(8,128)}), f32[32,16,128]{2,1,0:T(8,128)S(1)}, u32[]{:S(2)}, u32[]{:S(2)}) %all-to-all-start.2) | async-done | bytes 262176 | tf_op jit(solution)/shard_map/all_to_all | solution.py:284
  45.4 0.0 copy-start
  45.4 1.1 gram_strips.1
  46.5 1.1 copy-done
  47.6 1.8 %sketch_rows.1 = (f32[8,128,256]{2,1,0:T(8,128)S(1)}, f32[8,128,256]{2,1,0:T(8,128)}) custom-call(s32[1]{0:T(128)} %bitcast.3.core_ref, f32[512,128]{1,0:T(8,128)S(1)} %bitcast.7, bf16[512,4096]{1,0:T(8,128)(2,1)S(1)} %copy-done), custom_call_target="tpu_custom_call" | custom-call | tf_op jit(solution)/shard_map/sketch_rows/pallas_call | solution.py:190
  49.4 5.5 %collective-permute-start.2 = (f32[8,128,256]{2,1,0:T(8,128)}, f32[8,128,256]{2,1,0:T(8,128)S(1)}, u32[]{:S(2)}, u32[]{:S(2)}) collective-permute-start(f32[8,128,256]{2,1,0:T(8,128)} %get-tuple-element.33), channel_id=1, source_target_pairs={{0,32},{32,0},{64,96},{96,64},{128,160},{160,128},{192,224},{224,1... | collective-permute-start | bytes 3145736 | tf_op jit(solution)/shard_map/ppermute | solution.py:290
  54.9 7.2 %all-to-all-start.3 = ((f32[16,32,128]{2,1,0:T(8,128)}), f32[16,32,128]{2,1,0:T(8,128)S(1)}, u32[]{:S(2)}, u32[]{:S(2)}) async-start(f32[16,32,128]{2,1,0:T(8,128)} %gram_strips.1), calls=%async_computation.3 | async-start | bytes 524288 | tf_op jit(solution)/shard_map/all_to_all | solution.py:288
  62.2 0.0 collective-permute-done.2.b_ref
  62.2 0.9 fold.1
  63.1 10.8 %all-to-all-done.3.parts_ref = f32[16,32,128]{2,1,0:T(8,128)S(1)} async-done(((f32[16,32,128]{2,1,0:T(8,128)}), f32[16,32,128]{2,1,0:T(8,128)S(1)}, u32[]{:S(2)}, u32[]{:S(2)}) %all-to-all-start.3) | async-done | bytes 262176 | tf_op jit(solution)/shard_map/all_to_all | solution.py:288
  73.9 3.5 %all-to-all-start.4 = ((bf16[8,128,256]{2,1,0:T(8,128)(2,1)}), bf16[8,128,256]{2,1,0:T(8,128)(2,1)S(1)}, u32[]{:S(2)}, u32[]{:S(2)}) async-start(bf16[8,128,256]{2,1,0:T(8,128)(2,1)} %get-tuple-element.35), calls=%async_computation.4 | async-start | bytes 1048576 | tf_op jit(solution)/shard_map/all_to_all | solution.py:274
  77.4 3.7 %collective-permute-start = (f32[1,32,128]{2,1,0:T(8,128)S(1)}, f32[1,32,128]{2,1,0:T(8,128)S(1)}, u32[]{:S(2)}, u32[]{:S(2)}) collective-permute-start(f32[1,32,128]{2,1,0:T(8,128)S(1)} %share.3), channel_id=1, source_target_pairs={{0,2},{1,3},{2,0},{3,1},{4,6},{5,7},{6,4},{7,5},{8,10},{9,11},{10,... | collective-permute-start | bytes 49160 | tf_op jit(solution)/shard_map/ppermute | solution.py:293
  81.1 2.1 %collective-permute-done = f32[1,32,128]{2,1,0:T(8,128)S(1)} collective-permute-done((f32[1,32,128]{2,1,0:T(8,128)S(1)}, f32[1,32,128]{2,1,0:T(8,128)S(1)}, u32[]{:S(2)}, u32[]{:S(2)}) %collective-permute-start) | collective-permute-done | bytes 16416 | tf_op jit(solution)/shard_map/ppermute | solution.py:293
  83.2 4.0 %collective-permute-start.1 = (f32[2,32,128]{2,1,0:T(8,128)S(1)}, f32[2,32,128]{2,1,0:T(8,128)S(1)}, u32[]{:S(2)}, u32[]{:S(2)}) collective-permute-start(f32[2,32,128]{2,1,0:T(8,128)S(1)} %pad_maximum_fusion.1), channel_id=1, source_target_pairs={{0,4},{1,5},{2,6},{3,7},{4,0},{5,1},{6,2},{7,3},{8,12},{9,13},{10,... | collective-permute-start | bytes 98312 | tf_op jit(solution)/shard_map/ppermute | solution.py:293
  87.2 4.6 %collective-permute-done.1 = f32[2,32,128]{2,1,0:T(8,128)S(1)} collective-permute-done((f32[2,32,128]{2,1,0:T(8,128)S(1)}, f32[2,32,128]{2,1,0:T(8,128)S(1)}, u32[]{:S(2)}, u32[]{:S(2)}) %collective-permute-start.1) | collective-permute-done | bytes 32800 | tf_op jit(solution)/shard_map/ppermute | solution.py:293
  91.9 4.3 %chol_inv.1 = (f32[128,128]{1,0:T(8,128)S(1)}, f32[8,128]{1,0:T(8,128)S(1)}) custom-call(s32[1]{0:T(128)} %bitcast.2.z_ref, f32[4,32,128]{2,1,0:T(8,128)S(1)} %pad_maximum_fusion.g_ref), custom_call_target="tpu_custom_call" | custom-call | tf_op jit(solution)/shard_map/chol_inv/pallas_call | solution.py:83
  96.2 0.6 reduce_sum.9
  97.5 0.0 all-to-all-done.4
  97.5 0.3 conditional.1
  97.5 0.3 finish.3
  97.8 20.7 %all_to_all.31.own_ref = bf16[8,128,256]{2,1,0:T(8,128)(2,1)S(1)} all-to-all(bf16[8,128,256]{2,1,0:T(8,128)(2,1)S(1)} %get-tuple-element.36), channel_id=1, replica_groups={{0,64,128,192,256,320,384,448},{32,96,160,224,288,352,416,480},{1,65,12..., dimensions={0} | all-to-all | bytes 1048576 | tf_op jit(solution)/shard_map/all_to_all | solution.py:274
  118.5 5.9 %collective-permute-start.3 = (bf16[8,128,256]{2,1,0:T(8,128)(2,1)S(1)}, bf16[8,128,256]{2,1,0:T(8,128)(2,1)S(1)}, u32[]{:S(2)}, u32[]{:S(2)}) collective-permute-start(bf16[8,128,256]{2,1,0:T(8,128)(2,1)S(1)} %all_to_all.31.own_ref), channel_id=1, source_target_pairs={{0,32},{32,0},{64,96},{96,64},{128,160},{160,128},{192,224},{224,1... | collective-permute-start | bytes 1572872 | tf_op jit(solution)/shard_map/ppermute | solution.py:304
  124.4 1.0 convolution_convert_fusion
  125.4 0.5 collective-permute-done.3.other_ref
  125.9 1.1 place.1
  (3 shorter events, 0.0 us)
Async XLA Ops:
  29.4 16.0 %all-to-all-start.2 = ((f32[32,16,128]{2,1,0:T(8,128)}), f32[32,16,128]{2,1,0:T(8,128)S(1)}, u32[]{:S(2)}, u32[]{:S(2)}) async-start(f32[32,16,128]{2,1,0:T(8,128)} %share.2), calls=%async_computation.2 | async-start | bytes 524288 | tf_op jit(solution)/shard_map/all_to_all | solution.py:284
  45.4 2.3 %copy-start = (bf16[512,4096]{1,0:T(8,128)(2,1)S(1)}, bf16[512,4096]{1,0:T(8,128)(2,1)}, u32[]{:S(2)}) copy-start(bf16[512,4096]{1,0:T(8,128)(2,1)} %m_ref.3) | copy-start | bytes 12582916
  49.4 12.7 %collective-permute-start.2 = (f32[8,128,256]{2,1,0:T(8,128)}, f32[8,128,256]{2,1,0:T(8,128)S(1)}, u32[]{:S(2)}, u32[]{:S(2)}) collective-permute-start(f32[8,128,256]{2,1,0:T(8,128)} %get-tuple-element.33), channel_id=1, source_target_pairs={{0,32},{32,0},{64,96},{96,64},{128,160},{160,128},{192,224},{224,1... | collective-permute-start | bytes 3145736 | tf_op jit(solution)/shard_map/ppermute | solution.py:290
  54.9 18.9 %all-to-all-start.3 = ((f32[16,32,128]{2,1,0:T(8,128)}), f32[16,32,128]{2,1,0:T(8,128)S(1)}, u32[]{:S(2)}, u32[]{:S(2)}) async-start(f32[16,32,128]{2,1,0:T(8,128)} %gram_strips.1), calls=%async_computation.3 | async-start | bytes 524288 | tf_op jit(solution)/shard_map/all_to_all | solution.py:288
  73.9 23.6 %all-to-all-start.4 = ((bf16[8,128,256]{2,1,0:T(8,128)(2,1)}), bf16[8,128,256]{2,1,0:T(8,128)(2,1)S(1)}, u32[]{:S(2)}, u32[]{:S(2)}) async-start(bf16[8,128,256]{2,1,0:T(8,128)(2,1)} %get-tuple-element.35), calls=%async_computation.4 | async-start | bytes 1048576 | tf_op jit(solution)/shard_map/all_to_all | solution.py:274
  77.4 5.8 %collective-permute-start = (f32[1,32,128]{2,1,0:T(8,128)S(1)}, f32[1,32,128]{2,1,0:T(8,128)S(1)}, u32[]{:S(2)}, u32[]{:S(2)}) collective-permute-start(f32[1,32,128]{2,1,0:T(8,128)S(1)} %share.3), channel_id=1, source_target_pairs={{0,2},{1,3},{2,0},{3,1},{4,6},{5,7},{6,4},{7,5},{8,10},{9,11},{10,... | collective-permute-start | bytes 49160 | tf_op jit(solution)/shard_map/ppermute | solution.py:293
  83.2 8.6 %collective-permute-start.1 = (f32[2,32,128]{2,1,0:T(8,128)S(1)}, f32[2,32,128]{2,1,0:T(8,128)S(1)}, u32[]{:S(2)}, u32[]{:S(2)}) collective-permute-start(f32[2,32,128]{2,1,0:T(8,128)S(1)} %pad_maximum_fusion.1), channel_id=1, source_target_pairs={{0,4},{1,5},{2,6},{3,7},{4,0},{5,1},{6,2},{7,3},{8,12},{9,13},{10,... | collective-permute-start | bytes 98312 | tf_op jit(solution)/shard_map/ppermute | solution.py:293
  118.5 7.4 %collective-permute-start.3 = (bf16[8,128,256]{2,1,0:T(8,128)(2,1)S(1)}, bf16[8,128,256]{2,1,0:T(8,128)(2,1)S(1)}, u32[]{:S(2)}, u32[]{:S(2)}) collective-permute-start(bf16[8,128,256]{2,1,0:T(8,128)(2,1)S(1)} %all_to_all.31.own_ref), channel_id=1, source_target_pairs={{0,32},{32,0},{64,96},{96,64},{128,160},{160,128},{192,224},{224,1... | collective-permute-start | bytes 1572872 | tf_op jit(solution)/shard_map/ppermute | solution.py:304

commit v5 on v4

--- a/solution.py
+++ b/solution.py
@@ -65,7 +65,7 @@
         done = jnp.where(lane <= lo + sub, u * lax.rsqrt(dvec), 0.0)
         o_ref[lo : lo + T, :] = done
         squares = squares + done * done
-    q_ref[...] = squares * jnp.sum(diagonal, axis=0, keepdims=True)
+    q_ref[0, 0] = jnp.sum(squares * jnp.sum(diagonal, axis=0, keepdims=True))
 
 
 HBM = pl.BlockSpec(memory_space=pltpu.HBM)
@@ -73,6 +73,7 @@
 SMEM = pl.BlockSpec(memory_space=pltpu.SMEM)
 STEPS = 4
 STRIPS = 4
+SWAPS = 2
 
 
 def scalar(value):
@@ -83,8 +84,8 @@
     return pl.pallas_call(
         chol_inv_kernel,
         in_specs=[SMEM, VMEM],
-        out_specs=[VMEM, VMEM],
-        out_shape=[jax.ShapeDtypeStruct((K, K), F32), jax.ShapeDtypeStruct((T, K), F32)],
+        out_specs=[VMEM, SMEM],
+        out_shape=[jax.ShapeDtypeStruct((K, K), F32), jax.ShapeDtypeStruct((1, 1), F32)],
         compiler_params=room(4),
         name="chol_inv",
     )(scalar(z), strips)
@@ -171,49 +172,63 @@
     )(scalar(z), sampled)
 
 
-def w_kernel(core_ref, s_ref, m_ref, own_ref, other_ref):
+def w_kernel(core_ref, s_ref, m_ref, own_ref, low_ref, *high_refs):
     turned = s_ref[...].T
     high = turned.astype(BF16)
     low = (turned - high.astype(F32)).astype(BF16)
     hl = jnp.concatenate([high, low], axis=0)
     width = own_ref.shape[2]
+    per = NY // SWAPS
     core = core_ref[0]
-    for half, out_ref in ((1 - core, other_ref), (core, own_ref)):
+    for half, mine in ((1 - core, False), (core, True)):
         for y in range(NY):
             at = pl.multiple_of((half * NY + y) * width, width)
             w = jnp.dot(hl, m_ref[:, pl.ds(at, width)], preferred_element_type=F32)
-            out_ref[y] = w[:K] + w[K:]
+            w = w[:K] + w[K:]
+            if mine:
+                own_ref[y] = w
+            else:
+                lead = w.astype(BF16)
+                high_refs[y // per][y % per] = lead
+                low_ref[y] = (w - lead.astype(F32)).astype(BF16)
 
 
 def sketch_rows(sampled, matrix, core):
     width = matrix.shape[1] // NROW
-    return pl.pallas_call(
+    own, low, *high = pl.pallas_call(
         w_kernel,
         in_specs=[SMEM, VMEM, VMEM],
-        out_specs=[VMEM, VMEM],
-        out_shape=[jax.ShapeDtypeStruct((NY, K, width), F32)] * 2,
+        out_specs=[VMEM] * (2 + SWAPS),
+        out_shape=[
+            jax.ShapeDtypeStruct((NY, K, width), F32),
+            jax.ShapeDtypeStruct((NY, K, width), BF16),
+        ]
+        + [jax.ShapeDtypeStruct((NY // SWAPS, K, width), BF16)] * SWAPS,
         compiler_params=room(20),
         name="sketch_rows",
     )(scalar(core), sampled, matrix)
-
-
-def fold_kernel(a_ref, b_ref, high_ref, low_ref):
+    return own, low, high
+
+
+def fold_kernel(a_ref, *refs):
+    high_ref, rest_ref = refs[-2:]
+    per = NY // SWAPS
     for y in range(NY):
-        w = a_ref[y] + b_ref[y]
+        w = a_ref[y] + refs[y // per][y % per].astype(F32)
         high = w.astype(BF16)
         high_ref[y] = high
-        low_ref[y] = (w - high.astype(F32)).astype(BF16)
-
-
-def fold(a, b):
+        rest_ref[y] = w - high.astype(F32)
+
+
+def fold(a, parts):
     return pl.pallas_call(
         fold_kernel,
-        in_specs=[VMEM, VMEM],
+        in_specs=[VMEM] * (1 + SWAPS),
         out_specs=[VMEM, VMEM],
-        out_shape=[jax.ShapeDtypeStruct(a.shape, BF16)] * 2,
+        out_shape=[jax.ShapeDtypeStruct(a.shape, BF16), jax.ShapeDtypeStruct(a.shape, F32)],
         compiler_params=room(8),
         name="fold",
-    )(a, b)
+    )(a, *parts)
 
 
 def finish_kernel(inv_ref, *refs):
@@ -286,18 +301,20 @@
     strips = gram_strips(sampled, z)
     held, strips = lax.optimization_barrier((sampled, strips))
     strips = share(lax.all_to_all(strips, "row", 0, 0), 1)
-    own, other = sketch_rows(held, matrix, core)
-    high, low = fold(own, lax.ppermute(other, "row", SWAP))
+    own, low, other = sketch_rows(held, matrix, core)
+    high, rest = fold(own, [lax.ppermute(part, "row", SWAP) for part in other])
     parts = over_y(high)
     for step in (2, 4):
         theirs = lax.ppermute(strips, "col", [(i, i ^ step) for i in range(NCOL)])
         strips = jnp.concatenate([strips, theirs], axis=0)
     inverse, growth = chol_inv(strips, z)
 
+    def with_residuals():
+        residual = (rest + lax.ppermute(low, "row", SWAP).astype(F32)).astype(BF16)
+        return finish(inverse, parts, over_y(residual))
+
     pieces = lax.cond(
-        jnp.sum(growth) <= 2.0 * K,
-        lambda: finish(inverse, parts),
-        lambda: finish(inverse, parts, over_y(low)),
+        growth[0, 0] <= 2.0 * K, lambda: finish(inverse, parts), with_residuals
     )
     pieces = over_y(pieces)
     basis = lax.dot_general(sampled, inverse, (((1,), (1,)), ((), ())), precision=HIGH).astype(BF16)

time: 128 us -> 124 us (0.969)
  waiting for transfers between devices: 27.6 us -> 19.7 us
  starting transfers between devices: 36.1 us -> 40.5 us
    all_to_all x1, waiting for transfers between devices: 10.8 us -> 1.81 us  [local(): strips = share(lax.all_to_all(strips, 'row', 0, 0), 1)]
    all_to_all x1, starting transfers between devices: 7.24 us -> 10.7 us  [local(): strips = share(lax.all_to_all(strips, 'row', 0, 0), 1)]
    all_to_all x1, starting transfers between devices: 3.49 us -> 5 us  [over_y(): return lax.all_to_all(blocks, 'row', 0, 0, axis_index_groups=Y_GROUPS)]
    ppermute x1 -> x2, starting transfers between devices: 5.49 us -> 4.33 us  [local(): high, rest = fold(own, [lax.ppermute(part, 'row', SWAP) for part in other])]
  transfers between devices with their start and end apart: 7 -> 8, of which waited for: 5 -> 6; matrix products, arithmetic and copies ran while one was open for 1% -> 1% of each run, Pallas kernels for 4% -> 6%
where the time goes in v5:
time: 124 us
  blocking collectives  43.7 us (35%)
  starting transfers between devices  40.5 us (33%)
  waiting for transfers between devices  19.7 us (16%)
  Pallas kernels  15.2 us (12%)
  local copies, waits for them, and re-layouts  2.18 us (2%)
  between operations  1.46 us (1%)
    all_to_all x1, blocking collectives, local(): lax.all_to_all(partial_value.reshape(NCOL, rows // NCOL, K), 'col', 0, 0)  23.4 us
    all_to_all x1, blocking collectives, over_y(): return lax.all_to_all(blocks, 'row', 0, 0, axis_index_groups=Y_GROUPS)  20.2 us
    all_to_all x1, starting transfers between devices, local(): strips = share(lax.all_to_all(strips, 'row', 0, 0), 1)  10.7 us
    all_to_all x1, waiting for transfers between devices, local(): sampled = lax.all_to_all(share(parts, NCOL), 'col', 0, 0).reshape(rows, K)  9.63 us
    ppermute x2, starting transfers between devices, local(): theirs = lax.ppermute(strips, 'col', [(i, i ^ step) for i in range(NCOL)])  7.37 us
    ppermute x1, starting transfers between devices, local(): return (basis, place(pieces, lax.ppermute(pieces, 'row', SWAP), core))  6.82 us
    ppermute x2, waiting for transfers between devices, local(): theirs = lax.ppermute(strips, 'col', [(i, i ^ step) for i in range(NCOL)])  6.65 us
    all_to_all x1, starting transfers between devices, local(): sampled = lax.all_to_all(share(parts, NCOL), 'col', 0, 0).reshape(rows, K)  6.29 us
  transfers between devices with their start and end apart: 8, of which 6 were waited for; matrix products, arithmetic and copies ran while one was open for 1% of the time, Pallas kernels for 6%

profile of v5, /device:TPU:1, one launch (start us, length us, event | category | flops | bytes accessed | tf_op | source)
XLA Modules:
  0.0 123.7 jit_solution(14819583609987929210)
XLA Ops:
  0.6 4.6 %sketch.1 = f32[512,128]{1,0:T(8,128)} custom-call(bf16[512,4096]{1,0:T(8,128)(2,1)} %m_ref.3, bf16[4096,128]{1,0:T(8,128)(2,1)} %o_ref.1), custom_call_target="tpu_custom_call" | custom-call | tf_op jit(solution)/shard_map/sketch/pallas_call | solution.py:116
  5.3 23.4 %all_to_all.30.parts_ref = f32[32,16,128]{2,1,0:T(8,128)S(1)} all-to-all(f32[32,16,128]{2,1,0:T(8,128)} %bitcast.10), channel_id=1, replica_groups=mesh['row'=16,'col'=32] {'col'}, dimensions={0} | all-to-all | bytes 524288 | tf_op jit(solution)/shard_map/all_to_all | solution.py:298
  28.7 0.7 share.2
  29.4 6.3 %all-to-all-start.2 = ((f32[32,16,128]{2,1,0:T(8,128)}), f32[32,16,128]{2,1,0:T(8,128)S(1)}, u32[]{:S(2)}, u32[]{:S(2)}) async-start(f32[32,16,128]{2,1,0:T(8,128)} %share.2), calls=%async_computation.2 | async-start | bytes 524288 | tf_op jit(solution)/shard_map/all_to_all | solution.py:299
  35.7 9.6 %all-to-all-done.2 = f32[32,16,128]{2,1,0:T(8,128)S(1)} async-done(((f32[32,16,128]{2,1,0:T(8,128)}), f32[32,16,128]{2,1,0:T(8,128)S(1)}, u32[]{:S(2)}, u32[]{:S(2)}) %all-to-all-start.2) | async-done | bytes 262176 | tf_op jit(solution)/shard_map/all_to_all | solution.py:299
  45.4 1.1 gram_strips.1
  46.5 10.7 %all-to-all-start.3 = ((f32[16,32,128]{2,1,0:T(8,128)}), f32[16,32,128]{2,1,0:T(8,128)S(1)}, u32[]{:S(2)}, u32[]{:S(2)}) async-start(f32[16,32,128]{2,1,0:T(8,128)} %gram_strips.1), calls=%async_computation.3 | async-start | bytes 524288 | tf_op jit(solution)/shard_map/all_to_all | solution.py:303
  57.2 0.0 copy-start
  57.2 2.2 %copy-done = bf16[512,4096]{1,0:T(8,128)(2,1)S(1)} copy-done((bf16[512,4096]{1,0:T(8,128)(2,1)S(1)}, bf16[512,4096]{1,0:T(8,128)(2,1)}, u32[]{:S(2)}) %copy-start) | copy-done | bytes 4194328
  59.4 1.3 %sketch_rows.1 = (f32[8,128,256]{2,1,0:T(8,128)S(1)}, bf16[8,128,256]{2,1,0:T(8,128)(2,1)S(1)}, bf16[4,128,256]{2,1,0:T(8,128)(2,1)S(1)}, bf16[4,128,256]{2,1,0:T(8,128)(2,1)S(1)}) custom-call(s32[1]{0:T(128)} %bitcast.3.core_ref, f32[512,128]{1,0:T(8,128)S(1)} %bitcast.8, bf16[512,4096]{1,0:T(8,128)(2,1)S(1)} %copy-done), custom_call_target="tpu_custom_call" | custom-call | tf_op jit(solution)/shard_map/sketch_rows/pallas_call | solution.py:198
  60.7 2.0 %collective-permute-start.3 = (bf16[4,128,256]{2,1,0:T(8,128)(2,1)S(1)}, bf16[4,128,256]{2,1,0:T(8,128)(2,1)S(1)}, u32[]{:S(2)}, u32[]{:S(2)}) collective-permute-start(bf16[4,128,256]{2,1,0:T(8,128)(2,1)S(1)} %get-tuple-element.39), channel_id=1, source_target_pairs={{0,32},{32,0},{64,96},{96,64},{128,160},{160,128},{192,224},{224,1... | collective-permute-start | bytes 786440 | tf_op jit(solution)/shard_map/ppermute | solution.py:305
  62.8 2.3 %collective-permute-start.4 = (bf16[4,128,256]{2,1,0:T(8,128)(2,1)S(1)}, bf16[4,128,256]{2,1,0:T(8,128)(2,1)S(1)}, u32[]{:S(2)}, u32[]{:S(2)}) collective-permute-start(bf16[4,128,256]{2,1,0:T(8,128)(2,1)S(1)} %get-tuple-element.40), channel_id=1, source_target_pairs={{0,32},{32,0},{64,96},{96,64},{128,160},{160,128},{192,224},{224,1... | collective-permute-start | bytes 786440 | tf_op jit(solution)/shard_map/ppermute | solution.py:305
  65.1 0.0 collective-permute-done.3.refs_0_
  65.1 1.1 collective-permute-done.4.refs_1_
  66.2 0.9 fold.1
  67.1 1.8 %all-to-all-done.3.parts_ref = f32[16,32,128]{2,1,0:T(8,128)S(1)} async-done(((f32[16,32,128]{2,1,0:T(8,128)}), f32[16,32,128]{2,1,0:T(8,128)S(1)}, u32[]{:S(2)}, u32[]{:S(2)}) %all-to-all-start.3) | async-done | bytes 262176 | tf_op jit(solution)/shard_map/all_to_all | solution.py:303
  68.9 5.0 %all-to-all-start.4 = ((bf16[8,128,256]{2,1,0:T(8,128)(2,1)}), bf16[8,128,256]{2,1,0:T(8,128)(2,1)S(1)}, u32[]{:S(2)}, u32[]{:S(2)}) async-start(bf16[8,128,256]{2,1,0:T(8,128)(2,1)} %get-tuple-element.42), calls=%async_computation.4 | async-start | bytes 1048576 | tf_op jit(solution)/shard_map/all_to_all | solution.py:289
  73.9 3.7 %collective-permute-start.1 = (f32[1,32,128]{2,1,0:T(8,128)S(1)}, f32[1,32,128]{2,1,0:T(8,128)S(1)}, u32[]{:S(2)}, u32[]{:S(2)}) collective-permute-start(f32[1,32,128]{2,1,0:T(8,128)S(1)} %share.3), channel_id=1, source_target_pairs={{0,2},{1,3},{2,0},{3,1},{4,6},{5,7},{6,4},{7,5},{8,10},{9,11},{10,... | collective-permute-start | bytes 49160 | tf_op jit(solution)/shard_map/ppermute | solution.py:308
  77.7 1.7 %collective-permute-done.1 = f32[1,32,128]{2,1,0:T(8,128)S(1)} collective-permute-done((f32[1,32,128]{2,1,0:T(8,128)S(1)}, f32[1,32,128]{2,1,0:T(8,128)S(1)}, u32[]{:S(2)}, u32[]{:S(2)}) %collective-permute-start.1) | collective-permute-done | bytes 16416 | tf_op jit(solution)/shard_map/ppermute | solution.py:308
  79.3 3.7 %collective-permute-start.2 = (f32[2,32,128]{2,1,0:T(8,128)S(1)}, f32[2,32,128]{2,1,0:T(8,128)S(1)}, u32[]{:S(2)}, u32[]{:S(2)}) collective-permute-start(f32[2,32,128]{2,1,0:T(8,128)S(1)} %pad_maximum_fusion.1), channel_id=1, source_target_pairs={{0,4},{1,5},{2,6},{3,7},{4,0},{5,1},{6,2},{7,3},{8,12},{9,13},{10,... | collective-permute-start | bytes 98312 | tf_op jit(solution)/shard_map/ppermute | solution.py:308
  83.0 5.0 %collective-permute-done.2 = f32[2,32,128]{2,1,0:T(8,128)S(1)} collective-permute-done((f32[2,32,128]{2,1,0:T(8,128)S(1)}, f32[2,32,128]{2,1,0:T(8,128)S(1)}, u32[]{:S(2)}, u32[]{:S(2)}) %collective-permute-start.2) | collective-permute-done | bytes 32800 | tf_op jit(solution)/shard_map/ppermute | solution.py:308
  88.0 5.0 %chol_inv.1 = (f32[128,128]{1,0:T(8,128)S(1)}, f32[1,1]{1,0:T(1,128)}) custom-call(s32[1]{0:T(128)} %bitcast.2.z_ref, f32[4,32,128]{2,1,0:T(8,128)S(1)} %pad_maximum_fusion.g_ref), custom_call_target="tpu_custom_call" | custom-call | tf_op jit(solution)/shard_map/chol_inv/pallas_call | solution.py:84
  93.7 0.0 all-to-all-done.4
  93.7 0.3 conditional.1
  93.7 0.3 finish.3
  94.1 20.2 %all_to_all.31.own_ref = bf16[8,128,256]{2,1,0:T(8,128)(2,1)S(1)} all-to-all(bf16[8,128,256]{2,1,0:T(8,128)(2,1)S(1)} %get-tuple-element.43), channel_id=1, replica_groups={{0,64,128,192,256,320,384,448},{32,96,160,224,288,352,416,480},{1,65,12..., dimensions={0} | all-to-all | bytes 1048576 | tf_op jit(solution)/shard_map/all_to_all | solution.py:289
  114.3 6.8 %collective-permute-start.5 = (bf16[8,128,256]{2,1,0:T(8,128)(2,1)S(1)}, bf16[8,128,256]{2,1,0:T(8,128)(2,1)S(1)}, u32[]{:S(2)}, u32[]{:S(2)}) collective-permute-start(bf16[8,128,256]{2,1,0:T(8,128)(2,1)S(1)} %all_to_all.31.own_ref), channel_id=1, source_target_pairs={{0,32},{32,0},{64,96},{96,64},{128,160},{160,128},{192,224},{224,1... | collective-permute-start | bytes 1572872 | tf_op jit(solution)/shard_map/ppermute | solution.py:321
  121.1 1.0 convolution_convert_fusion
  122.2 0.5 collective-permute-done.5.other_ref
  122.6 1.1 place.1
  (3 shorter events, 0.0 us)
Async XLA Ops:
  29.4 16.0 %all-to-all-start.2 = ((f32[32,16,128]{2,1,0:T(8,128)}), f32[32,16,128]{2,1,0:T(8,128)S(1)}, u32[]{:S(2)}, u32[]{:S(2)}) async-start(f32[32,16,128]{2,1,0:T(8,128)} %share.2), calls=%async_computation.2 | async-start | bytes 524288 | tf_op jit(solution)/shard_map/all_to_all | solution.py:299
  46.5 22.4 %all-to-all-start.3 = ((f32[16,32,128]{2,1,0:T(8,128)}), f32[16,32,128]{2,1,0:T(8,128)S(1)}, u32[]{:S(2)}, u32[]{:S(2)}) async-start(f32[16,32,128]{2,1,0:T(8,128)} %gram_strips.1), calls=%async_computation.3 | async-start | bytes 524288 | tf_op jit(solution)/shard_map/all_to_all | solution.py:303
  57.2 2.2 %copy-start = (bf16[512,4096]{1,0:T(8,128)(2,1)S(1)}, bf16[512,4096]{1,0:T(8,128)(2,1)}, u32[]{:S(2)}) copy-start(bf16[512,4096]{1,0:T(8,128)(2,1)} %m_ref.3) | copy-start | bytes 12582916
  60.7 4.3 %collective-permute-start.3 = (bf16[4,128,256]{2,1,0:T(8,128)(2,1)S(1)}, bf16[4,128,256]{2,1,0:T(8,128)(2,1)S(1)}, u32[]{:S(2)}, u32[]{:S(2)}) collective-permute-start(bf16[4,128,256]{2,1,0:T(8,128)(2,1)S(1)} %get-tuple-element.39), channel_id=1, source_target_pairs={{0,32},{32,0},{64,96},{96,64},{128,160},{160,128},{192,224},{224,1... | collective-permute-start | bytes 786440 | tf_op jit(solution)/shard_map/ppermute | solution.py:305
  62.8 3.5 %collective-permute-start.4 = (bf16[4,128,256]{2,1,0:T(8,128)(2,1)S(1)}, bf16[4,128,256]{2,1,0:T(8,128)(2,1)S(1)}, u32[]{:S(2)}, u32[]{:S(2)}) collective-permute-start(bf16[4,128,256]{2,1,0:T(8,128)(2,1)S(1)} %get-tuple-element.40), channel_id=1, source_target_pairs={{0,32},{32,0},{64,96},{96,64},{128,160},{160,128},{192,224},{224,1... | collective-permute-start | bytes 786440 | tf_op jit(solution)/shard_map/ppermute | solution.py:305
  68.9 24.8 %all-to-all-start.4 = ((bf16[8,128,256]{2,1,0:T(8,128)(2,1)}), bf16[8,128,256]{2,1,0:T(8,128)(2,1)S(1)}, u32[]{:S(2)}, u32[]{:S(2)}) async-start(bf16[8,128,256]{2,1,0:T(8,128)(2,1)} %get-tuple-element.42), calls=%async_computation.4 | async-start | bytes 1048576 | tf_op jit(solution)/shard_map/all_to_all | solution.py:289
  73.9 5.4 %collective-permute-start.1 = (f32[1,32,128]{2,1,0:T(8,128)S(1)}, f32[1,32,128]{2,1,0:T(8,128)S(1)}, u32[]{:S(2)}, u32[]{:S(2)}) collective-permute-start(f32[1,32,128]{2,1,0:T(8,128)S(1)} %share.3), channel_id=1, source_target_pairs={{0,2},{1,3},{2,0},{3,1},{4,6},{5,7},{6,4},{7,5},{8,10},{9,11},{10,... | collective-permute-start | bytes 49160 | tf_op jit(solution)/shard_map/ppermute | solution.py:308
  79.3 8.7 %collective-permute-start.2 = (f32[2,32,128]{2,1,0:T(8,128)S(1)}, f32[2,32,128]{2,1,0:T(8,128)S(1)}, u32[]{:S(2)}, u32[]{:S(2)}) collective-permute-start(f32[2,32,128]{2,1,0:T(8,128)S(1)} %pad_maximum_fusion.1), channel_id=1, source_target_pairs={{0,4},{1,5},{2,6},{3,7},{4,0},{5,1},{6,2},{7,3},{8,12},{9,13},{10,... | collective-permute-start | bytes 98312 | tf_op jit(solution)/shard_map/ppermute | solution.py:308
  114.3 8.3 %collective-permute-start.5 = (bf16[8,128,256]{2,1,0:T(8,128)(2,1)S(1)}, bf16[8,128,256]{2,1,0:T(8,128)(2,1)S(1)}, u32[]{:S(2)}, u32[]{:S(2)}) collective-permute-start(bf16[8,128,256]{2,1,0:T(8,128)(2,1)S(1)} %all_to_all.31.own_ref), channel_id=1, source_target_pairs={{0,32},{32,0},{64,96},{96,64},{128,160},{160,128},{192,224},{224,1... | collective-permute-start | bytes 1572872 | tf_op jit(solution)/shard_map/ppermute | solution.py:321

commit v6 on v5

--- a/solution.py
+++ b/solution.py
@@ -27,12 +27,12 @@
     return jnp.broadcast_to(x[:, i : i + 1], (T, K))
 
 
-def chol_inv_kernel(z_ref, g_ref, o_ref, q_ref):
-    z = z_ref[0]
+def chol_inv_kernel(x_ref, g_ref, o_ref, q_ref):
+    mine = x_ref[0]
     sub = lax.broadcasted_iota(jnp.int32, (T, K), 0)
     lane = lax.broadcasted_iota(jnp.int32, (T, K), 1)
     per = g_ref.shape[1] // T
-    a = [g_ref[(p // per) ^ z, (p % per) * T : (p % per + 1) * T, :] for p in range(NP)]
+    a = [g_ref[(p // per) ^ mine, (p % per) * T : (p % per + 1) * T, :] for p in range(NP)]
     squares = jnp.zeros((T, K), F32)
     diagonal = jnp.zeros((T, K), F32)
     for p in range(NP):
@@ -80,7 +80,7 @@
     return value.astype(jnp.int32).reshape(1)
 
 
-def chol_inv(strips, z):
+def chol_inv(strips, x):
     return pl.pallas_call(
         chol_inv_kernel,
         in_specs=[SMEM, VMEM],
@@ -88,7 +88,7 @@
         out_shape=[jax.ShapeDtypeStruct((K, K), F32), jax.ShapeDtypeStruct((1, 1), F32)],
         compiler_params=room(4),
         name="chol_inv",
-    )(scalar(z), strips)
+    )(scalar(x), strips)
 
 
 def sketch_kernel(m_ref, o_ref, p_ref, held, omega, m_sems, o_sems):
@@ -149,17 +149,17 @@
     )(parts)
 
 
-def gram_kernel(z_ref, s_ref, out_ref, held):
+def gram_kernel(x_ref, s_ref, out_ref, held):
     held[...] = lax.dot_general(
         s_ref[...], s_ref[...], (((0,), (0,)), ((), ())), precision=HIGH, preferred_element_type=F32
     )
     tall = out_ref.shape[1]
-    strip = held[pl.ds(pl.multiple_of(z_ref[0] * tall, tall), tall), :]
+    strip = held[pl.ds(pl.multiple_of(x_ref[0] * tall, tall), tall), :]
     for k in range(NROW):
         out_ref[k] = strip
 
 
-def gram_strips(sampled, z):
+def gram_strips(sampled, x):
     return pl.pallas_call(
         gram_kernel,
         in_specs=[SMEM, VMEM],
@@ -169,28 +169,30 @@
         compiler_params=room(8),
         cost_estimate=pl.CostEstimate(flops=2_500_000_000, bytes_accessed=8 << 20, transcendentals=0),
         name="gram_strips",
-    )(scalar(z), sampled)
+    )(scalar(x), sampled)
 
 
 def w_kernel(core_ref, s_ref, m_ref, own_ref, low_ref, *high_refs):
     turned = s_ref[...].T
-    high = turned.astype(BF16)
-    low = (turned - high.astype(F32)).astype(BF16)
-    hl = jnp.concatenate([high, low], axis=0)
+    terms = []
+    for _ in range(3):
+        terms.append(turned.astype(BF16))
+        turned = turned - terms[-1].astype(F32)
+    terms = jnp.concatenate(terms, axis=0)
     width = own_ref.shape[2]
     per = NY // SWAPS
     core = core_ref[0]
     for half, mine in ((1 - core, False), (core, True)):
         for y in range(NY):
             at = pl.multiple_of((half * NY + y) * width, width)
-            w = jnp.dot(hl, m_ref[:, pl.ds(at, width)], preferred_element_type=F32)
-            w = w[:K] + w[K:]
+            w = jnp.dot(terms, m_ref[:, pl.ds(at, width)], preferred_element_type=F32)
+            w = w[:K] + (w[K : 2 * K] + w[2 * K :])
             if mine:
                 own_ref[y] = w
             else:
                 lead = w.astype(BF16)
                 high_refs[y // per][y % per] = lead
-                low_ref[y] = (w - lead.astype(F32)).astype(BF16)
+                low_ref[y] = w - lead.astype(F32)
 
 
 def sketch_rows(sampled, matrix, core):
@@ -201,7 +203,7 @@
         out_specs=[VMEM] * (2 + SWAPS),
         out_shape=[
             jax.ShapeDtypeStruct((NY, K, width), F32),
-            jax.ShapeDtypeStruct((NY, K, width), BF16),
+            jax.ShapeDtypeStruct((NY, K, width), F32),
         ]
         + [jax.ShapeDtypeStruct((NY // SWAPS, K, width), BF16)] * SWAPS,
         compiler_params=room(20),
@@ -291,27 +293,26 @@
 
 def local(matrix, omega):
     core = lax.axis_index("row") % 2
-    z = lax.axis_index("col") % NZ // 2
+    x = lax.axis_index("col") // NZ
     rows = matrix.shape[0]
 
     partial_value = sketch(matrix, omega)
     parts = lax.all_to_all(partial_value.reshape(NCOL, rows // NCOL, K), "col", 0, 0)
     sampled = lax.all_to_all(share(parts, NCOL), "col", 0, 0).reshape(rows, K)
 
-    strips = gram_strips(sampled, z)
+    strips = gram_strips(sampled, x)
     held, strips = lax.optimization_barrier((sampled, strips))
     strips = share(lax.all_to_all(strips, "row", 0, 0), 1)
     own, low, other = sketch_rows(held, matrix, core)
     high, rest = fold(own, [lax.ppermute(part, "row", SWAP) for part in other])
     parts = over_y(high)
-    for step in (2, 4):
+    for step in (NZ, 2 * NZ):
         theirs = lax.ppermute(strips, "col", [(i, i ^ step) for i in range(NCOL)])
         strips = jnp.concatenate([strips, theirs], axis=0)
-    inverse, growth = chol_inv(strips, z)
+    inverse, growth = chol_inv(strips, x)
 
     def with_residuals():
-        residual = (rest + lax.ppermute(low, "row", SWAP).astype(F32)).astype(BF16)
-        return finish(inverse, parts, over_y(residual))
+        return finish(inverse, parts, over_y(rest + lax.ppermute(low, "row", SWAP)))
 
     pieces = lax.cond(
         growth[0, 0] <= 2.0 * K, lambda: finish(inverse, parts), with_residuals

time: 124 us -> 122 us (0.984)
  starting transfers between devices: 40.5 us -> 38.3 us
    ppermute x2, starting transfers between devices: 7.37 us -> 5.47 us  [local(): theirs = lax.ppermute(strips, 'col', [(i, i ^ step) for i in range(NCOL)])]
  transfers between devices with their start and end apart: 8 -> 8, of which waited for: 6 -> 7; matrix products, arithmetic and copies ran while one was open for 1% -> 1% of each run, Pallas kernels for 6% -> 6%
where the time goes in v6:
time: 122 us; the launch traced here: 121 us
  blocking collectives  43.2 us (35%)
  starting transfers between devices  38.3 us (31%)
  waiting for transfers between devices  19.3 us (16%)
  Pallas kernels  15.7 us (13%)
  local copies, waits for them, and re-layouts  2.18 us (2%)
  between operations  1.44 us (1%)
    all_to_all x1, blocking collectives, local(): lax.all_to_all(partial_value.reshape(NCOL, rows // NCOL, K), 'col', 0, 0)  23.4 us
    all_to_all x1, blocking collectives, over_y(): return lax.all_to_all(blocks, 'row', 0, 0, axis_index_groups=Y_GROUPS)  19.8 us
    all_to_all x1, starting transfers between devices, local(): strips = share(lax.all_to_all(strips, 'row', 0, 0), 1)  10.7 us
    all_to_all x1, waiting for transfers between devices, local(): sampled = lax.all_to_all(share(parts, NCOL), 'col', 0, 0).reshape(rows, K)  9.64 us
    all_to_all x1, starting transfers between devices, local(): sampled = lax.all_to_all(share(parts, NCOL), 'col', 0, 0).reshape(rows, K)  6.29 us
    ppermute x1, starting transfers between devices, local(): return (basis, place(pieces, lax.ppermute(pieces, 'row', SWAP), core))  6.02 us
    ppermute x2, waiting for transfers between devices, local(): theirs = lax.ppermute(strips, 'col', [(i, i ^ step) for i in range(NCOL)])  5.74 us
    all_to_all x1, starting transfers between devices, over_y(): return lax.all_to_all(blocks, 'row', 0, 0, axis_index_groups=Y_GROUPS)  5.52 us
  transfers between devices with their start and end apart: 8, of which 7 were waited for; matrix products, arithmetic and copies ran while one was open for 1% of the time, Pallas kernels for 6%

profile of v6, /device:TPU:1, one launch (start us, length us, event | category | flops | bytes accessed | tf_op | source)
XLA Modules:
  0.0 121.2 jit_solution(12530540778708551337)
XLA Ops:
  0.6 4.6 %sketch.1 = f32[512,128]{1,0:T(8,128)} custom-call(bf16[512,4096]{1,0:T(8,128)(2,1)} %m_ref.3, bf16[4096,128]{1,0:T(8,128)(2,1)} %o_ref.1), custom_call_target="tpu_custom_call" | custom-call | tf_op jit(solution)/shard_map/sketch/pallas_call | solution.py:116
  5.3 23.4 %all_to_all.30.parts_ref = f32[32,16,128]{2,1,0:T(8,128)S(1)} all-to-all(f32[32,16,128]{2,1,0:T(8,128)} %bitcast.10), channel_id=1, replica_groups=mesh['row'=16,'col'=32] {'col'}, dimensions={0} | all-to-all | bytes 524288 | tf_op jit(solution)/shard_map/all_to_all | solution.py:300
  28.7 0.7 share.2
  29.4 6.3 %all-to-all-start.2 = ((f32[32,16,128]{2,1,0:T(8,128)}), f32[32,16,128]{2,1,0:T(8,128)S(1)}, u32[]{:S(2)}, u32[]{:S(2)}) async-start(f32[32,16,128]{2,1,0:T(8,128)} %share.2), calls=%async_computation.2 | async-start | bytes 524288 | tf_op jit(solution)/shard_map/all_to_all | solution.py:301
  35.7 9.6 %all-to-all-done.2 = f32[32,16,128]{2,1,0:T(8,128)S(1)} async-done(((f32[32,16,128]{2,1,0:T(8,128)}), f32[32,16,128]{2,1,0:T(8,128)S(1)}, u32[]{:S(2)}, u32[]{:S(2)}) %all-to-all-start.2) | async-done | bytes 262176 | tf_op jit(solution)/shard_map/all_to_all | solution.py:301
  45.4 1.1 gram_strips.1
  46.5 10.7 %all-to-all-start.3 = ((f32[16,32,128]{2,1,0:T(8,128)}), f32[16,32,128]{2,1,0:T(8,128)S(1)}, u32[]{:S(2)}, u32[]{:S(2)}) async-start(f32[16,32,128]{2,1,0:T(8,128)} %gram_strips.1), calls=%async_computation.3 | async-start | bytes 524288 | tf_op jit(solution)/shard_map/all_to_all | solution.py:305
  57.2 0.0 copy-start
  57.2 2.2 %copy-done = bf16[512,4096]{1,0:T(8,128)(2,1)S(1)} copy-done((bf16[512,4096]{1,0:T(8,128)(2,1)S(1)}, bf16[512,4096]{1,0:T(8,128)(2,1)}, u32[]{:S(2)}) %copy-start) | copy-done | bytes 4194328
  59.4 1.9 %sketch_rows.1 = (f32[8,128,256]{2,1,0:T(8,128)S(1)}, f32[8,128,256]{2,1,0:T(8,128)S(1)}, bf16[4,128,256]{2,1,0:T(8,128)(2,1)S(1)}, bf16[4,128,256]{2,1,0:T(8,128)(2,1)S(1)}) custom-call(s32[1]{0:T(128)} %bitcast.3.core_ref, f32[512,128]{1,0:T(8,128)S(1)} %bitcast.8, bf16[512,4096]{1,0:T(8,128)(2,1)S(1)} %copy-done), custom_call_target="tpu_custom_call" | custom-call | tf_op jit(solution)/shard_map/sketch_rows/pallas_call | solution.py:200
  61.3 2.0 %collective-permute-start.3 = (bf16[4,128,256]{2,1,0:T(8,128)(2,1)S(1)}, bf16[4,128,256]{2,1,0:T(8,128)(2,1)S(1)}, u32[]{:S(2)}, u32[]{:S(2)}) collective-permute-start(bf16[4,128,256]{2,1,0:T(8,128)(2,1)S(1)} %get-tuple-element.39), channel_id=1, source_target_pairs={{0,32},{32,0},{64,96},{96,64},{128,160},{160,128},{192,224},{224,1... | collective-permute-start | bytes 786440 | tf_op jit(solution)/shard_map/ppermute | solution.py:307
  63.3 2.3 %collective-permute-start.4 = (bf16[4,128,256]{2,1,0:T(8,128)(2,1)S(1)}, bf16[4,128,256]{2,1,0:T(8,128)(2,1)S(1)}, u32[]{:S(2)}, u32[]{:S(2)}) collective-permute-start(bf16[4,128,256]{2,1,0:T(8,128)(2,1)S(1)} %get-tuple-element.40), channel_id=1, source_target_pairs={{0,32},{32,0},{64,96},{96,64},{128,160},{160,128},{192,224},{224,1... | collective-permute-start | bytes 786440 | tf_op jit(solution)/shard_map/ppermute | solution.py:307
  65.6 0.0 collective-permute-done.3.refs_0_
  65.6 1.1 collective-permute-done.4.refs_1_
  66.8 0.9 fold.1
  67.6 1.3 %all-to-all-done.3.parts_ref = f32[16,32,128]{2,1,0:T(8,128)S(1)} async-done(((f32[16,32,128]{2,1,0:T(8,128)}), f32[16,32,128]{2,1,0:T(8,128)S(1)}, u32[]{:S(2)}, u32[]{:S(2)}) %all-to-all-start.3) | async-done | bytes 262176 | tf_op jit(solution)/shard_map/all_to_all | solution.py:305
  68.9 5.5 %all-to-all-start.4 = ((bf16[8,128,256]{2,1,0:T(8,128)(2,1)}), bf16[8,128,256]{2,1,0:T(8,128)(2,1)S(1)}, u32[]{:S(2)}, u32[]{:S(2)}) async-start(bf16[8,128,256]{2,1,0:T(8,128)(2,1)} %get-tuple-element.42), calls=%async_computation.4 | async-start | bytes 1048576 | tf_op jit(solution)/shard_map/all_to_all | solution.py:291
  74.5 2.2 %collective-permute-start.1 = (f32[1,32,128]{2,1,0:T(8,128)S(1)}, f32[1,32,128]{2,1,0:T(8,128)S(1)}, u32[]{:S(2)}, u32[]{:S(2)}) collective-permute-start(f32[1,32,128]{2,1,0:T(8,128)S(1)} %share.3), channel_id=1, source_target_pairs={{0,8},{1,9},{2,10},{3,11},{4,12},{5,13},{6,14},{7,15},{8,0},{9,1},... | collective-permute-start | bytes 49160 | tf_op jit(solution)/shard_map/ppermute | solution.py:310
  76.7 2.5 %collective-permute-done.1 = f32[1,32,128]{2,1,0:T(8,128)S(1)} collective-permute-done((f32[1,32,128]{2,1,0:T(8,128)S(1)}, f32[1,32,128]{2,1,0:T(8,128)S(1)}, u32[]{:S(2)}, u32[]{:S(2)}) %collective-permute-start.1) | collective-permute-done | bytes 16416 | tf_op jit(solution)/shard_map/ppermute | solution.py:310
  79.3 3.2 %collective-permute-start.2 = (f32[2,32,128]{2,1,0:T(8,128)S(1)}, f32[2,32,128]{2,1,0:T(8,128)S(1)}, u32[]{:S(2)}, u32[]{:S(2)}) collective-permute-start(f32[2,32,128]{2,1,0:T(8,128)S(1)} %pad_maximum_fusion.1), channel_id=1, source_target_pairs={{0,16},{1,17},{2,18},{3,19},{4,20},{5,21},{6,22},{7,23},{8,24},{9,... | collective-permute-start | bytes 98312 | tf_op jit(solution)/shard_map/ppermute | solution.py:310
  82.5 3.2 %collective-permute-done.2 = f32[2,32,128]{2,1,0:T(8,128)S(1)} collective-permute-done((f32[2,32,128]{2,1,0:T(8,128)S(1)}, f32[2,32,128]{2,1,0:T(8,128)S(1)}, u32[]{:S(2)}, u32[]{:S(2)}) %collective-permute-start.2) | collective-permute-done | bytes 32800 | tf_op jit(solution)/shard_map/ppermute | solution.py:310
  85.7 5.0 %chol_inv.1 = (f32[128,128]{1,0:T(8,128)S(1)}, f32[1,1]{1,0:T(1,128)}) custom-call(s32[1]{0:T(128)} %bitcast.2.x_ref, f32[4,32,128]{2,1,0:T(8,128)S(1)} %pad_maximum_fusion.g_ref), custom_call_target="tpu_custom_call" | custom-call | tf_op jit(solution)/shard_map/chol_inv/pallas_call | solution.py:84
  91.4 1.0 all-to-all-done.4
  92.4 0.3 conditional.1
  92.4 0.3 finish.3
  92.7 19.8 %all_to_all.31.own_ref = bf16[8,128,256]{2,1,0:T(8,128)(2,1)S(1)} all-to-all(bf16[8,128,256]{2,1,0:T(8,128)(2,1)S(1)} %get-tuple-element.43), channel_id=1, replica_groups={{0,64,128,192,256,320,384,448},{32,96,160,224,288,352,416,480},{1,65,12..., dimensions={0} | all-to-all | bytes 1048576 | tf_op jit(solution)/shard_map/all_to_all | solution.py:291
  112.6 6.0 %collective-permute-start.5 = (bf16[8,128,256]{2,1,0:T(8,128)(2,1)S(1)}, bf16[8,128,256]{2,1,0:T(8,128)(2,1)S(1)}, u32[]{:S(2)}, u32[]{:S(2)}) collective-permute-start(bf16[8,128,256]{2,1,0:T(8,128)(2,1)S(1)} %all_to_all.31.own_ref), channel_id=1, source_target_pairs={{0,32},{32,0},{64,96},{96,64},{128,160},{160,128},{192,224},{224,1... | collective-permute-start | bytes 1572872 | tf_op jit(solution)/shard_map/ppermute | solution.py:322
  118.6 1.0 convolution_convert_fusion
  119.6 0.5 collective-permute-done.5.other_ref
  120.1 1.1 place.1
  (3 shorter events, 0.0 us)
Async XLA Ops:
  29.4 16.0 %all-to-all-start.2 = ((f32[32,16,128]{2,1,0:T(8,128)}), f32[32,16,128]{2,1,0:T(8,128)S(1)}, u32[]{:S(2)}, u32[]{:S(2)}) async-start(f32[32,16,128]{2,1,0:T(8,128)} %share.2), calls=%async_computation.2 | async-start | bytes 524288 | tf_op jit(solution)/shard_map/all_to_all | solution.py:301
  46.5 22.4 %all-to-all-start.3 = ((f32[16,32,128]{2,1,0:T(8,128)}), f32[16,32,128]{2,1,0:T(8,128)S(1)}, u32[]{:S(2)}, u32[]{:S(2)}) async-start(f32[16,32,128]{2,1,0:T(8,128)} %gram_strips.1), calls=%async_computation.3 | async-start | bytes 524288 | tf_op jit(solution)/shard_map/all_to_all | solution.py:305
  57.2 2.2 %copy-start = (bf16[512,4096]{1,0:T(8,128)(2,1)S(1)}, bf16[512,4096]{1,0:T(8,128)(2,1)}, u32[]{:S(2)}) copy-start(bf16[512,4096]{1,0:T(8,128)(2,1)} %m_ref.3) | copy-start | bytes 12582916
  61.3 4.3 %collective-permute-start.3 = (bf16[4,128,256]{2,1,0:T(8,128)(2,1)S(1)}, bf16[4,128,256]{2,1,0:T(8,128)(2,1)S(1)}, u32[]{:S(2)}, u32[]{:S(2)}) collective-permute-start(bf16[4,128,256]{2,1,0:T(8,128)(2,1)S(1)} %get-tuple-element.39), channel_id=1, source_target_pairs={{0,32},{32,0},{64,96},{96,64},{128,160},{160,128},{192,224},{224,1... | collective-permute-start | bytes 786440 | tf_op jit(solution)/shard_map/ppermute | solution.py:307
  63.3 3.5 %collective-permute-start.4 = (bf16[4,128,256]{2,1,0:T(8,128)(2,1)S(1)}, bf16[4,128,256]{2,1,0:T(8,128)(2,1)S(1)}, u32[]{:S(2)}, u32[]{:S(2)}) collective-permute-start(bf16[4,128,256]{2,1,0:T(8,128)(2,1)S(1)} %get-tuple-element.40), channel_id=1, source_target_pairs={{0,32},{32,0},{64,96},{96,64},{128,160},{160,128},{192,224},{224,1... | collective-permute-start | bytes 786440 | tf_op jit(solution)/shard_map/ppermute | solution.py:307
  68.9 23.5 %all-to-all-start.4 = ((bf16[8,128,256]{2,1,0:T(8,128)(2,1)}), bf16[8,128,256]{2,1,0:T(8,128)(2,1)S(1)}, u32[]{:S(2)}, u32[]{:S(2)}) async-start(bf16[8,128,256]{2,1,0:T(8,128)(2,1)} %get-tuple-element.42), calls=%async_computation.4 | async-start | bytes 1048576 | tf_op jit(solution)/shard_map/all_to_all | solution.py:291
  74.5 4.8 %collective-permute-start.1 = (f32[1,32,128]{2,1,0:T(8,128)S(1)}, f32[1,32,128]{2,1,0:T(8,128)S(1)}, u32[]{:S(2)}, u32[]{:S(2)}) collective-permute-start(f32[1,32,128]{2,1,0:T(8,128)S(1)} %share.3), channel_id=1, source_target_pairs={{0,8},{1,9},{2,10},{3,11},{4,12},{5,13},{6,14},{7,15},{8,0},{9,1},... | collective-permute-start | bytes 49160 | tf_op jit(solution)/shard_map/ppermute | solution.py:310
  79.3 6.4 %collective-permute-start.2 = (f32[2,32,128]{2,1,0:T(8,128)S(1)}, f32[2,32,128]{2,1,0:T(8,128)S(1)}, u32[]{:S(2)}, u32[]{:S(2)}) collective-permute-start(f32[2,32,128]{2,1,0:T(8,128)S(1)} %pad_maximum_fusion.1), channel_id=1, source_target_pairs={{0,16},{1,17},{2,18},{3,19},{4,20},{5,21},{6,22},{7,23},{8,24},{9,... | collective-permute-start | bytes 98312 | tf_op jit(solution)/shard_map/ppermute | solution.py:310
  112.6 7.5 %collective-permute-start.5 = (bf16[8,128,256]{2,1,0:T(8,128)(2,1)S(1)}, bf16[8,128,256]{2,1,0:T(8,128)(2,1)S(1)}, u32[]{:S(2)}, u32[]{:S(2)}) collective-permute-start(bf16[8,128,256]{2,1,0:T(8,128)(2,1)S(1)} %all_to_all.31.own_ref), channel_id=1, source_target_pairs={{0,32},{32,0},{64,96},{96,64},{128,160},{160,128},{192,224},{224,1... | collective-permute-start | bytes 1572872 | tf_op jit(solution)/shard_map/ppermute | solution.py:322

commit v7 on v6

--- a/solution.py
+++ b/solution.py
@@ -27,12 +27,14 @@
     return jnp.broadcast_to(x[:, i : i + 1], (T, K))
 
 
-def chol_inv_kernel(x_ref, g_ref, o_ref, q_ref):
-    mine = x_ref[0]
+def chol_inv_kernel(x_ref, *refs):
+    o_ref, q_ref, held = refs[STRIPS:]
+    for j in range(STRIPS):
+        held[j ^ x_ref[0]] = refs[j][0]
     sub = lax.broadcasted_iota(jnp.int32, (T, K), 0)
     lane = lax.broadcasted_iota(jnp.int32, (T, K), 1)
-    per = g_ref.shape[1] // T
-    a = [g_ref[(p // per) ^ mine, (p % per) * T : (p % per + 1) * T, :] for p in range(NP)]
+    per = NP // STRIPS
+    a = [held[p // per, (p % per) * T : (p % per + 1) * T, :] for p in range(NP)]
     squares = jnp.zeros((T, K), F32)
     diagonal = jnp.zeros((T, K), F32)
     for p in range(NP):
@@ -83,12 +85,13 @@
 def chol_inv(strips, x):
     return pl.pallas_call(
         chol_inv_kernel,
-        in_specs=[SMEM, VMEM],
+        in_specs=[SMEM] + [VMEM] * STRIPS,
         out_specs=[VMEM, SMEM],
         out_shape=[jax.ShapeDtypeStruct((K, K), F32), jax.ShapeDtypeStruct((1, 1), F32)],
+        scratch_shapes=[pltpu.VMEM((STRIPS, K // STRIPS, K), F32)],
         compiler_params=room(4),
         name="chol_inv",
-    )(scalar(x), strips)
+    )(scalar(x), *strips)
 
 
 def sketch_kernel(m_ref, o_ref, p_ref, held, omega, m_sems, o_sems):
@@ -306,9 +309,10 @@
     own, low, other = sketch_rows(held, matrix, core)
     high, rest = fold(own, [lax.ppermute(part, "row", SWAP) for part in other])
     parts = over_y(high)
-    for step in (NZ, 2 * NZ):
-        theirs = lax.ppermute(strips, "col", [(i, i ^ step) for i in range(NCOL)])
-        strips = jnp.concatenate([strips, theirs], axis=0)
+    strips = [strips] + [
+        lax.ppermute(strips, "col", [(i, i ^ (j * NZ)) for i in range(NCOL)])
+        for j in range(1, STRIPS)
+    ]
     inverse, growth = chol_inv(strips, x)
 
     def with_residuals():

time: 122 us -> 121 us (level)
  waiting for transfers between devices: 19.3 us -> 15.7 us
  starting transfers between devices: 38.3 us -> 41.7 us
    ppermute x2 -> x3, waiting for transfers between devices: 5.74 us -> 1.73 us  [local(): lax.ppermute(strips, 'col', [(i, i ^ j * NZ) for i in range(NCOL)])]
    ppermute x2 -> x3, starting transfers between devices: 5.47 us -> 8.98 us  [local(): lax.ppermute(strips, 'col', [(i, i ^ j * NZ) for i in range(NCOL)])]
  transfers between devices with their start and end apart: 8 -> 9, of which waited for: 7 -> 7; matrix products, arithmetic and copies ran while one was open for 1% -> 1% of each run, Pallas kernels for 6% -> 6%
where the time goes in v7:
time: 121 us
  blocking collectives  42.8 us (35%)
  starting transfers between devices  41.7 us (34%)
  Pallas kernels  15.7 us (13%)
  waiting for transfers between devices  15.7 us (13%)
  local copies, waits for them, and re-layouts  2.18 us (2%)
  between operations  1.45 us (1%)
    all_to_all x1, blocking collectives, local(): lax.all_to_all(partial_value.reshape(NCOL, rows // NCOL, K), 'col', 0, 0)  23.4 us
    all_to_all x1, blocking collectives, over_y(): return lax.all_to_all(blocks, 'row', 0, 0, axis_index_groups=Y_GROUPS)  19.4 us
    all_to_all x1, starting transfers between devices, local(): strips = share(lax.all_to_all(strips, 'row', 0, 0), 1)  10.7 us
    all_to_all x1, waiting for transfers between devices, local(): sampled = lax.all_to_all(share(parts, NCOL), 'col', 0, 0).reshape(rows, K)  9.64 us
    ppermute x3, starting transfers between devices, local(): lax.ppermute(strips, 'col', [(i, i ^ j * NZ) for i in range(NCOL)])  8.98 us
    all_to_all x1, starting transfers between devices, local(): sampled = lax.all_to_all(share(parts, NCOL), 'col', 0, 0).reshape(rows, K)  6.29 us
    ppermute x1, starting transfers between devices, local(): return (basis, place(pieces, lax.ppermute(pieces, 'row', SWAP), core))  5.9 us
    all_to_all x1, starting transfers between devices, over_y(): return lax.all_to_all(blocks, 'row', 0, 0, axis_index_groups=Y_GROUPS)  5.52 us
  transfers between devices with their start and end apart: 9, of which 7 were waited for; matrix products, arithmetic and copies ran while one was open for 1% of the time, Pallas kernels for 6%

profile of v7, /device:TPU:1, one launch (start us, length us, event | category | flops | bytes accessed | tf_op | source)
XLA Modules:
  0.0 120.7 jit_solution(14231683168052375618)
XLA Ops:
  0.6 4.6 %sketch.1 = f32[512,128]{1,0:T(8,128)} custom-call(bf16[512,4096]{1,0:T(8,128)(2,1)} %m_ref.3, bf16[4096,128]{1,0:T(8,128)(2,1)} %o_ref.1), custom_call_target="tpu_custom_call" | custom-call | tf_op jit(solution)/shard_map/sketch/pallas_call | solution.py:119
  5.3 23.4 %all_to_all.30.parts_ref = f32[32,16,128]{2,1,0:T(8,128)S(1)} all-to-all(f32[32,16,128]{2,1,0:T(8,128)} %bitcast.10), channel_id=1, replica_groups=mesh['row'=16,'col'=32] {'col'}, dimensions={0} | all-to-all | bytes 524288 | tf_op jit(solution)/shard_map/all_to_all | solution.py:303
  28.7 0.7 share.2
  29.4 6.3 %all-to-all-start.2 = ((f32[32,16,128]{2,1,0:T(8,128)}), f32[32,16,128]{2,1,0:T(8,128)S(1)}, u32[]{:S(2)}, u32[]{:S(2)}) async-start(f32[32,16,128]{2,1,0:T(8,128)} %share.2), calls=%async_computation.2 | async-start | bytes 524288 | tf_op jit(solution)/shard_map/all_to_all | solution.py:304
  35.7 9.6 %all-to-all-done.2 = f32[32,16,128]{2,1,0:T(8,128)S(1)} async-done(((f32[32,16,128]{2,1,0:T(8,128)}), f32[32,16,128]{2,1,0:T(8,128)S(1)}, u32[]{:S(2)}, u32[]{:S(2)}) %all-to-all-start.2) | async-done | bytes 262176 | tf_op jit(solution)/shard_map/all_to_all | solution.py:304
  45.4 1.1 gram_strips.1
  46.5 10.7 %all-to-all-start.3 = ((f32[16,32,128]{2,1,0:T(8,128)}), f32[16,32,128]{2,1,0:T(8,128)S(1)}, u32[]{:S(2)}, u32[]{:S(2)}) async-start(f32[16,32,128]{2,1,0:T(8,128)} %gram_strips.1), calls=%async_computation.3 | async-start | bytes 524288 | tf_op jit(solution)/shard_map/all_to_all | solution.py:308
  57.2 0.0 copy-start
  57.2 2.2 %copy-done = bf16[512,4096]{1,0:T(8,128)(2,1)S(1)} copy-done((bf16[512,4096]{1,0:T(8,128)(2,1)S(1)}, bf16[512,4096]{1,0:T(8,128)(2,1)}, u32[]{:S(2)}) %copy-start) | copy-done | bytes 4194328
  59.4 1.9 %sketch_rows.1 = (f32[8,128,256]{2,1,0:T(8,128)S(1)}, f32[8,128,256]{2,1,0:T(8,128)S(1)}, bf16[4,128,256]{2,1,0:T(8,128)(2,1)S(1)}, bf16[4,128,256]{2,1,0:T(8,128)(2,1)S(1)}) custom-call(s32[1]{0:T(128)} %bitcast.3.core_ref, f32[512,128]{1,0:T(8,128)S(1)} %bitcast.8, bf16[512,4096]{1,0:T(8,128)(2,1)S(1)} %copy-done), custom_call_target="tpu_custom_call" | custom-call | tf_op jit(solution)/shard_map/sketch_rows/pallas_call | solution.py:203
  61.3 2.0 %collective-permute-start.4 = (bf16[4,128,256]{2,1,0:T(8,128)(2,1)S(1)}, bf16[4,128,256]{2,1,0:T(8,128)(2,1)S(1)}, u32[]{:S(2)}, u32[]{:S(2)}) collective-permute-start(bf16[4,128,256]{2,1,0:T(8,128)(2,1)S(1)} %get-tuple-element.39), channel_id=1, source_target_pairs={{0,32},{32,0},{64,96},{96,64},{128,160},{160,128},{192,224},{224,1... | collective-permute-start | bytes 786440 | tf_op jit(solution)/shard_map/ppermute | solution.py:310
  63.3 2.3 %collective-permute-start.5 = (bf16[4,128,256]{2,1,0:T(8,128)(2,1)S(1)}, bf16[4,128,256]{2,1,0:T(8,128)(2,1)S(1)}, u32[]{:S(2)}, u32[]{:S(2)}) collective-permute-start(bf16[4,128,256]{2,1,0:T(8,128)(2,1)S(1)} %get-tuple-element.40), channel_id=1, source_target_pairs={{0,32},{32,0},{64,96},{96,64},{128,160},{160,128},{192,224},{224,1... | collective-permute-start | bytes 786440 | tf_op jit(solution)/shard_map/ppermute | solution.py:310
  65.6 0.0 collective-permute-done.4.refs_0_
  65.6 1.1 collective-permute-done.5.refs_1_
  66.7 0.9 fold.1
  67.6 1.3 %all-to-all-done.3.parts_ref = f32[16,32,128]{2,1,0:T(8,128)S(1)} async-done(((f32[16,32,128]{2,1,0:T(8,128)}), f32[16,32,128]{2,1,0:T(8,128)S(1)}, u32[]{:S(2)}, u32[]{:S(2)}) %all-to-all-start.3) | async-done | bytes 262176 | tf_op jit(solution)/shard_map/all_to_all | solution.py:308
  68.9 5.5 %all-to-all-start.4 = ((bf16[8,128,256]{2,1,0:T(8,128)(2,1)}), bf16[8,128,256]{2,1,0:T(8,128)(2,1)S(1)}, u32[]{:S(2)}, u32[]{:S(2)}) async-start(bf16[8,128,256]{2,1,0:T(8,128)(2,1)} %get-tuple-element.42), calls=%async_computation.4 | async-start | bytes 1048576 | tf_op jit(solution)/shard_map/all_to_all | solution.py:294
  74.5 3.0 %collective-permute-start.3 = (f32[1,32,128]{2,1,0:T(8,128)S(1)}, f32[1,32,128]{2,1,0:T(8,128)S(1)}, u32[]{:S(2)}, u32[]{:S(2)}) collective-permute-start(f32[1,32,128]{2,1,0:T(8,128)S(1)} %share.3.refs_0_), channel_id=1, source_target_pairs={{0,24},{1,25},{2,26},{3,27},{4,28},{5,29},{6,30},{7,31},{8,16},{9,... | collective-permute-start | bytes 49160 | tf_op jit(solution)/shard_map/ppermute | solution.py:313
  77.4 3.0 %collective-permute-start.2 = (f32[1,32,128]{2,1,0:T(8,128)S(1)}, f32[1,32,128]{2,1,0:T(8,128)S(1)}, u32[]{:S(2)}, u32[]{:S(2)}) collective-permute-start(f32[1,32,128]{2,1,0:T(8,128)S(1)} %share.3.refs_0_), channel_id=1, source_target_pairs={{0,16},{1,17},{2,18},{3,19},{4,20},{5,21},{6,22},{7,23},{8,24},{9,... | collective-permute-start | bytes 49160 | tf_op jit(solution)/shard_map/ppermute | solution.py:313
  80.4 3.0 %collective-permute-start.1 = (f32[1,32,128]{2,1,0:T(8,128)S(1)}, f32[1,32,128]{2,1,0:T(8,128)S(1)}, u32[]{:S(2)}, u32[]{:S(2)}) collective-permute-start(f32[1,32,128]{2,1,0:T(8,128)S(1)} %share.3.refs_0_), channel_id=1, source_target_pairs={{0,8},{1,9},{2,10},{3,11},{4,12},{5,13},{6,14},{7,15},{8,0},{9,1},... | collective-permute-start | bytes 49160 | tf_op jit(solution)/shard_map/ppermute | solution.py:313
  83.5 0.0 collective-permute-done.3.refs_3_
  83.5 0.2 collective-permute-done.2.refs_2_
  83.7 1.5 %collective-permute-done.1.refs_1_ = f32[1,32,128]{2,1,0:T(8,128)S(1)} collective-permute-done((f32[1,32,128]{2,1,0:T(8,128)S(1)}, f32[1,32,128]{2,1,0:T(8,128)S(1)}, u32[]{:S(2)}, u32[]{:S(2)}) %collective-permute-start.1) | collective-permute-done | bytes 16416 | tf_op jit(solution)/shard_map/ppermute | solution.py:313
  85.2 5.0 %chol_inv.1 = (f32[128,128]{1,0:T(8,128)S(1)}, f32[1,1]{1,0:T(1,128)}) custom-call(s32[1]{0:T(128)} %bitcast.2.x_ref, f32[1,32,128]{2,1,0:T(8,128)S(1)} %share.3.refs_0_, f32[1,32,128]{2,1,0:T(8,128)S(1)} %collective-permute-done.1.refs_1_, f32[1,32,128]{2,1,0:T(8,128)S(1)} %collective-permute-done.2.refs_2_, f32[1,32,128]{2,1,0:T(8,128)S(1)} %collective-permute-done.3.refs_3_), custom_call_target="tpu_custom_call" | custom-call | tf_op jit(solution)/shard_map/chol_inv/pallas_call | solution.py:86
  90.9 1.5 %all-to-all-done.4 = bf16[8,128,256]{2,1,0:T(8,128)(2,1)S(1)} async-done(((bf16[8,128,256]{2,1,0:T(8,128)(2,1)}), bf16[8,128,256]{2,1,0:T(8,128)(2,1)S(1)}, u32[]{:S(2)}, u32[]{:S(2)}) %all-to-all-start.4) | async-done | bytes 524320 | tf_op jit(solution)/shard_map/all_to_all | solution.py:294
  92.4 0.3 conditional.1
  92.4 0.3 finish.3
  92.7 19.4 %all_to_all.31.own_ref = bf16[8,128,256]{2,1,0:T(8,128)(2,1)S(1)} all-to-all(bf16[8,128,256]{2,1,0:T(8,128)(2,1)S(1)} %get-tuple-element.43), channel_id=1, replica_groups={{0,64,128,192,256,320,384,448},{32,96,160,224,288,352,416,480},{1,65,12..., dimensions={0} | all-to-all | bytes 1048576 | tf_op jit(solution)/shard_map/all_to_all | solution.py:294
  112.2 5.9 %collective-permute-start.6 = (bf16[8,128,256]{2,1,0:T(8,128)(2,1)S(1)}, bf16[8,128,256]{2,1,0:T(8,128)(2,1)S(1)}, u32[]{:S(2)}, u32[]{:S(2)}) collective-permute-start(bf16[8,128,256]{2,1,0:T(8,128)(2,1)S(1)} %all_to_all.31.own_ref), channel_id=1, source_target_pairs={{0,32},{32,0},{64,96},{96,64},{128,160},{160,128},{192,224},{224,1... | collective-permute-start | bytes 1572872 | tf_op jit(solution)/shard_map/ppermute | solution.py:326
  118.1 1.0 convolution_convert_fusion
  119.1 0.5 collective-permute-done.6.other_ref
  119.6 1.1 place.1
  (1 shorter events, 0.0 us)
Async XLA Ops:
  29.4 16.0 %all-to-all-start.2 = ((f32[32,16,128]{2,1,0:T(8,128)}), f32[32,16,128]{2,1,0:T(8,128)S(1)}, u32[]{:S(2)}, u32[]{:S(2)}) async-start(f32[32,16,128]{2,1,0:T(8,128)} %share.2), calls=%async_computation.2 | async-start | bytes 524288 | tf_op jit(solution)/shard_map/all_to_all | solution.py:304
  46.5 22.4 %all-to-all-start.3 = ((f32[16,32,128]{2,1,0:T(8,128)}), f32[16,32,128]{2,1,0:T(8,128)S(1)}, u32[]{:S(2)}, u32[]{:S(2)}) async-start(f32[16,32,128]{2,1,0:T(8,128)} %gram_strips.1), calls=%async_computation.3 | async-start | bytes 524288 | tf_op jit(solution)/shard_map/all_to_all | solution.py:308
  57.2 2.2 %copy-start = (bf16[512,4096]{1,0:T(8,128)(2,1)S(1)}, bf16[512,4096]{1,0:T(8,128)(2,1)}, u32[]{:S(2)}) copy-start(bf16[512,4096]{1,0:T(8,128)(2,1)} %m_ref.3) | copy-start | bytes 12582916
  61.3 4.3 %collective-permute-start.4 = (bf16[4,128,256]{2,1,0:T(8,128)(2,1)S(1)}, bf16[4,128,256]{2,1,0:T(8,128)(2,1)S(1)}, u32[]{:S(2)}, u32[]{:S(2)}) collective-permute-start(bf16[4,128,256]{2,1,0:T(8,128)(2,1)S(1)} %get-tuple-element.39), channel_id=1, source_target_pairs={{0,32},{32,0},{64,96},{96,64},{128,160},{160,128},{192,224},{224,1... | collective-permute-start | bytes 786440 | tf_op jit(solution)/shard_map/ppermute | solution.py:310
  63.3 3.5 %collective-permute-start.5 = (bf16[4,128,256]{2,1,0:T(8,128)(2,1)S(1)}, bf16[4,128,256]{2,1,0:T(8,128)(2,1)S(1)}, u32[]{:S(2)}, u32[]{:S(2)}) collective-permute-start(bf16[4,128,256]{2,1,0:T(8,128)(2,1)S(1)} %get-tuple-element.40), channel_id=1, source_target_pairs={{0,32},{32,0},{64,96},{96,64},{128,160},{160,128},{192,224},{224,1... | collective-permute-start | bytes 786440 | tf_op jit(solution)/shard_map/ppermute | solution.py:310
  68.9 23.5 %all-to-all-start.4 = ((bf16[8,128,256]{2,1,0:T(8,128)(2,1)}), bf16[8,128,256]{2,1,0:T(8,128)(2,1)S(1)}, u32[]{:S(2)}, u32[]{:S(2)}) async-start(bf16[8,128,256]{2,1,0:T(8,128)(2,1)} %get-tuple-element.42), calls=%async_computation.4 | async-start | bytes 1048576 | tf_op jit(solution)/shard_map/all_to_all | solution.py:294
  74.5 9.0 %collective-permute-start.3 = (f32[1,32,128]{2,1,0:T(8,128)S(1)}, f32[1,32,128]{2,1,0:T(8,128)S(1)}, u32[]{:S(2)}, u32[]{:S(2)}) collective-permute-start(f32[1,32,128]{2,1,0:T(8,128)S(1)} %share.3.refs_0_), channel_id=1, source_target_pairs={{0,24},{1,25},{2,26},{3,27},{4,28},{5,29},{6,30},{7,31},{8,16},{9,... | collective-permute-start | bytes 49160 | tf_op jit(solution)/shard_map/ppermute | solution.py:313
  77.4 6.3 %collective-permute-start.2 = (f32[1,32,128]{2,1,0:T(8,128)S(1)}, f32[1,32,128]{2,1,0:T(8,128)S(1)}, u32[]{:S(2)}, u32[]{:S(2)}) collective-permute-start(f32[1,32,128]{2,1,0:T(8,128)S(1)} %share.3.refs_0_), channel_id=1, source_target_pairs={{0,16},{1,17},{2,18},{3,19},{4,20},{5,21},{6,22},{7,23},{8,24},{9,... | collective-permute-start | bytes 49160 | tf_op jit(solution)/shard_map/ppermute | solution.py:313
  80.4 4.8 %collective-permute-start.1 = (f32[1,32,128]{2,1,0:T(8,128)S(1)}, f32[1,32,128]{2,1,0:T(8,128)S(1)}, u32[]{:S(2)}, u32[]{:S(2)}) collective-permute-start(f32[1,32,128]{2,1,0:T(8,128)S(1)} %share.3.refs_0_), channel_id=1, source_target_pairs={{0,8},{1,9},{2,10},{3,11},{4,12},{5,13},{6,14},{7,15},{8,0},{9,1},... | collective-permute-start | bytes 49160 | tf_op jit(solution)/shard_map/ppermute | solution.py:313
  112.2 7.4 %collective-permute-start.6 = (bf16[8,128,256]{2,1,0:T(8,128)(2,1)S(1)}, bf16[8,128,256]{2,1,0:T(8,128)(2,1)S(1)}, u32[]{:S(2)}, u32[]{:S(2)}) collective-permute-start(bf16[8,128,256]{2,1,0:T(8,128)(2,1)S(1)} %all_to_all.31.own_ref), channel_id=1, source_target_pairs={{0,32},{32,0},{64,96},{96,64},{128,160},{160,128},{192,224},{224,1... | collective-permute-start | bytes 1572872 | tf_op jit(solution)/shard_map/ppermute | solution.py:326
